TPU v7x, 32 devices: a whole 2x2x4 slice. The times are simulated.
32 devices in a mesh: slab: 16 (over z, y, x), tile: 2 (over core).
Axes of the slice: x: 2, y: 2, z: 4, core: 2. Of those that a mesh axis runs over, the one named last changes fastest.
Arguments:
- samples: float32 [16, 64, 32, 256], P('slab', None, 'tile'), may hold values from -6 to 6
- counts: int32 [16, 64, 32], P('slab', None, 'tile'), may hold values from 1 to 4
- w_in: float32 [16, 64, 256], P('slab'), may hold values from -0.75 to 0.75
- b_in: float32 [16, 256], P('slab'), may hold values from -3 to 3
- w_color: float32 [16, 256, 128], P('slab'), may hold values from -0.375 to 0.375
- b_color: float32 [16, 128], P('slab'), may hold values from -3 to 3
- w_density: float32 [16, 256], P('slab'), may hold values from -0.375 to 0.375
- b_density: float32 [16], P('slab'), may hold values from -1 to 1
- conv_a: bfloat16 [3, 3, 128, 128], replicated, may hold values from -0.1875 to 0.1875
- bias_a: float32 [128], replicated, may hold values from -3 to 3
- conv_b: bfloat16 [3, 3, 128, 128], replicated, may hold values from -0.1875 to 0.1875
- bias_b: float32 [128], replicated, may hold values from -3 to 3
Outputs:
- decoded: bfloat16 [64, 32, 128], P('slab', 'tile')
- front: float32 [16, 64, 32], P('slab', None, 'tile')
All inputs are finite; a program needn't handle non-finite values.
Results may differ from a plain program's by a relative error of at most 0.006.
Values may be sent and summed in bfloat16 or wider, within the bound.
A program may use at most 128 MiB of HBM per device.

v0:
```python
import jax
import jax.numpy as jnp
from jax import lax
from jax.sharding import PartitionSpec as P

F = 64
K = 4


def padded_2(cells, sides, width):
    for axis, dim in sides:
        count = lax.axis_size(axis)
        ends = count - 1
        head = lax.slice_in_dim(cells, 0, width, axis=dim)
        tail = lax.slice_in_dim(cells, cells.shape[dim] - width, cells.shape[dim], axis=dim)
        cells = jnp.concatenate(
            [
                lax.ppermute(tail, axis, [(i, (i + 1) % count) for i in range(ends)]),
                cells,
                lax.ppermute(head, axis, [((i + 1) % count, i) for i in range(ends)]),
            ],
            axis=dim,
        )
    return cells


def prefix_2(part, axis, combine, identity):
    place = lax.axis_index(axis)
    gathered = lax.all_gather(part, axis)
    state = jnp.zeros_like(part) + jnp.asarray(identity, part.dtype)

    def one(turn, state):
        return combine(state, lax.dynamic_index_in_dim(gathered, turn, 0, False))

    return lax.fori_loop(0, place, one, state)


def as_sent(value):
    return jax.tree.map(lambda a: a.astype(jnp.bfloat16) if a.dtype == jnp.float32 else a, value)


def hidden_units(inputs, w_in, b_in):
    shaped = inputs.reshape(inputs.shape[:-1] + (K, F))
    return jax.nn.relu(
        jnp.einsum("rwkf,fh->rwkh", shaped, w_in, precision=lax.Precision.HIGHEST) + b_in
    )


def densities(hidden_act, w_density, b_density, live_count):
    before = (
        jnp.einsum("rwkh,h->rwk", hidden_act, w_density, precision=lax.Precision.HIGHEST)
        + b_density
    )
    slots = lax.broadcasted_iota(jnp.int32, before.shape, 2)
    return jnp.where(slots < live_count[..., None], jax.nn.softplus(before), 0.0)


def sample_weights(density, front, total):
    scaled = density / total[..., None]
    earlier = jnp.cumsum(scaled, axis=2) - scaled
    return jnp.exp(-front[..., None] - earlier) * (1.0 - jnp.exp(-scaled))


def partial_image(hidden_act, weight, w_color, b_color):
    color = (
        jnp.einsum("rwkh,hc->rwkc", hidden_act, w_color, precision=lax.Precision.HIGHEST) + b_color
    )
    return jnp.einsum("rwk,rwkc->rwc", weight, color, precision=lax.Precision.HIGHEST)


def add_pair(earlier, later):
    return earlier + later


def convolve(padded, kernel, out_rows, out_cols):
    result = jnp.zeros((out_rows, out_cols, kernel.shape[3]), jnp.float32)
    for row_shift in range(3):
        for col_shift in range(3):
            window = padded[row_shift : row_shift + out_rows, col_shift : col_shift + out_cols]
            result = result + jnp.einsum(
                "rwc,cd->rwd",
                window,
                kernel[row_shift, col_shift],
                preferred_element_type=jnp.float32,
            )
    return result


def strip_edges(field):
    return padded_2(field, (("slab", 0), ("tile", 1)), 1)


def body(
    samples,
    counts,
    w_in,
    b_in,
    w_color,
    b_color,
    w_density,
    b_density,
    conv_a,
    bias_a,
    conv_b,
    bias_b,
):
    slab_count = lax.axis_size("slab")
    height = samples.shape[1]
    tile_cols = samples.shape[2]
    strip_rows = height // slab_count
    hidden_act = hidden_units(samples[0], w_in[0], b_in[0])
    density = densities(hidden_act, w_density[0], b_density[0], counts[0])
    depth = jnp.sum(density, axis=2)
    prefix = prefix_2(depth, "slab", add_pair, jnp.zeros_like(depth))
    total = lax.psum(depth, "slab")
    front = prefix / total
    weight = sample_weights(density, front, total)
    whole_term = partial_image(hidden_act, weight, w_color[0], b_color[0])
    blocked = whole_term.reshape(slab_count, strip_rows, tile_cols, whole_term.shape[2])
    received = lax.all_to_all(
        as_sent(blocked), "slab", split_axis=0, concat_axis=0, tiled=True
    ).astype(blocked.dtype)
    image = jnp.sum(received, axis=0).astype(jnp.bfloat16)
    first_pad = strip_edges(image)
    hidden_map = jax.nn.relu(convolve(first_pad, conv_a, strip_rows, tile_cols) + bias_a).astype(
        jnp.bfloat16
    )
    second_pad = strip_edges(hidden_map)
    decoded = (convolve(second_pad, conv_b, strip_rows, tile_cols) + bias_b).astype(jnp.bfloat16)
    return (decoded, front[None])


def solution(mesh):
    in_specs = (
        P("slab", None, "tile", None),
        P("slab", None, "tile"),
        P("slab", None, None),
        P("slab", None),
        P("slab", None, None),
        P("slab", None),
        P("slab", None),
        P("slab"),
        P(),
        P(),
        P(),
        P(),
    )
    out_specs = (P("slab", "tile", None), P("slab", None, "tile"))
    return jax.shard_map(body, mesh=mesh, in_specs=in_specs, out_specs=out_specs, check_vma=False)
```

profile of v0, /device:TPU:9, one launch (start us, length us, event | category | flops | bytes accessed | tf_op | source)
XLA Modules:
  0.0 158.4 jit_solution(18078430850779183278)
XLA Ops:
  1.4 2.1 %reshape_squeeze.3 = f32[64,16,4,64]{3,2,1,0:T(4,128)S(1)} reshape(f32[1,64,16,256]{3,2,1,0:T(8,128)} %param.14) | data formatting | bytes 2097152 | tf_op jit(solution)/shard_map/reshape;squeeze | solution.py:43
  3.5 4.4 %fusion.2 = f32[64,16,4,256]{3,1,2,0:T(8,128)S(1)} fusion(f32[64,16,4,64]{3,2,1,0:T(4,128)S(1)} %reshape_squeeze.3, f32[1,64,256]{2,1,0:T(8,128)} %param.16), kind=kOutput, calls=%fused_computation.4 | convolution fusion | flops 805306368 | bytes 5308416 | tf_op jit(solution)/shard_map/rwkf,fh->rwkh/dot_general | solution.py:45
  7.9 1.9 %copy-done.1 = f32[64,16,4,256]{3,1,2,0:T(8,128)} copy-done((f32[64,16,4,256]{3,1,2,0:T(8,128)}, f32[64,16,4,256]{3,1,2,0:T(8,128)S(1)}, u32[]{:S(2)}) %copy-start.1) | copy-done | bytes 4194328
  9.8 14.7 %fusion.1 = f32[1,64,16,4]{2,0,3,1:T(1,128)S(1)} fusion(f32[64,16,4,256]{3,1,2,0:T(8,128)S(1)} %fusion.2, f32[256]{0:T(256)S(1)} %bitcast.148, f32[1,256]{1,0:T(1,128)S(1)} %copy-done.6), kind=kOutput, calls=%fused_computation.3 | convolution fusion | flops 14680064 | bytes 4212736 | tf_op jit(solution)/shard_map/rwkh,h->rwk/dot_general | solution.py:51
  24.7 28.9 %psum.7 = f32[64,16]{0,1:T(8,128)S(1)} all-reduce(f32[64,16]{0,1:T(8,128)S(1)} %fusion.112), channel_id=1, replica_groups=mesh['slab'=16,'tile'=2] {'slab'}, use_global_device_ids=true, to_apply=%region_3.4 | all-reduce | flops 1024 | bytes 8192 | tf_op jit(solution)/shard_map/psum | solution.py:115
  53.6 29.8 %all-gather.1 = f32[16,64,16]{1,2,0:T(8,128)S(1)} all-gather(f32[1,64,16]{1,2,0:T(8,128)S(1)} %bitcast.145), channel_id=2, replica_groups=mesh['slab'=16,'tile'=2] {'slab'}, dimensions={0}, use_global_device_ids=true | all-gather | bytes 69632 | tf_op jit(solution)/shard_map/all_gather | solution.py:29
  83.4 0.6 divide_bitcast_fusion
  84.1 0.6 copy.27
  84.7 5.3 %fusion.10 = f32[64,16,4,128]{3,1,2,0:T(8,128)S(1)} fusion(f32[64,16,4,256]{3,1,2,0:T(8,128)} %copy-done.1, f32[256]{0:T(256)S(1)} %bitcast.149, f32[128]{0:T(128)S(1)} %bitcast.150, f32[1,256,128]{2,1,0:T(8,128)S(1)} %copy-done), kind=kOutput, calls=%fused_computation.12 | convolution fusion | flops 1613234176 | bytes 6424064 | tf_op jit(solution)/shard_map/rwkh,hc->rwkc/dot_general | solution.py:66
  90.0 7.3 %fusion.8 = f32[64,16,1,128]{3,2,1,0:T(1,128)S(1)} fusion(f32[64,16,4,1]{2,3,1,0:T(1,128)S(1)} %copy.27, f32[64,16,4,128]{3,1,2,0:T(8,128)S(1)} %fusion.10), kind=kOutput, calls=%fused_computation.10 | convolution fusion | flops 6291456 | bytes 2637824 | tf_op jit(solution)/shard_map/rwk,rwkc->rwc/dot_general | solution.py:68
  97.4 15.7 %all_to_all.5 = bf16[16,4,16,128]{3,2,1,0:T(8,128)(2,1)S(1)} all-to-all(bf16[16,4,16,128]{3,2,1,0:T(8,128)(2,1)S(1)} %bitcast.143), channel_id=1, replica_groups=mesh['slab'=16,'tile'=2] {'slab'}, dimensions={0} | all-to-all | bytes 524288 | tf_op jit(solution)/shard_map/all_to_all | solution.py:120
  113.1 2.2 %collective-permute-start = (bf16[1,16,128]{2,1,0:T(8,128)(2,1)S(1)}, bf16[1,16,128]{2,1,0:T(8,128)(2,1)S(1)}, u32[]{:S(2)}, u32[]{:S(2)}) collective-permute-start(bf16[1,16,128]{2,1,0:T(8,128)(2,1)S(1)} %get-tuple-element.46), channel_id=1, source_target_pairs={{0,2},{2,4},{4,6},{6,8},{8,10},{10,12},{12,14},{14,16},{16,18},{18... | collective-permute-start | bytes 12296 | tf_op jit(solution)/shard_map/ppermute | solution.py:18
  115.3 4.9 %collective-permute-start.1 = (bf16[1,16,128]{2,1,0:T(8,128)(2,1)S(1)}, bf16[1,16,128]{2,1,0:T(8,128)(2,1)S(1)}, u32[]{:S(2)}, u32[]{:S(2)}) collective-permute-start(bf16[1,16,128]{2,1,0:T(8,128)(2,1)S(1)} %get-tuple-element.47), channel_id=1, source_target_pairs={{2,0},{4,2},{6,4},{8,6},{10,8},{12,10},{14,12},{16,14},{18,16},{20... | collective-permute-start | bytes 12296 | tf_op jit(solution)/shard_map/ppermute | solution.py:20
  120.3 0.6 collective-permute-done.1
  121.0 1.3 collective-permute-start.2
  122.3 19.4 %collective-permute-start.3 = (bf16[6,1,128]{2,1,0:T(2,128)(2,1)S(1)}, bf16[6,1,128]{2,1,0:T(2,128)(2,1)S(1)}, u32[]{:S(2)}, u32[]{:S(2)}) collective-permute-start(bf16[6,1,128]{2,1,0:T(2,128)(2,1)S(1)} %get-tuple-element.41), channel_id=1, source_target_pairs={{1,0},{3,2},{5,4},{7,6},{9,8},{11,10},{13,12},{15,14},{17,16},{19,... | collective-permute-start | bytes 4616 | tf_op jit(solution)/shard_map/ppermute | solution.py:20
  141.9 0.5 collective-permute-done.3
  143.3 3.5 %collective-permute-start.4 = (bf16[1,16,128]{2,1,0:T(8,128)(2,1)S(1)}, bf16[1,16,128]{2,1,0:T(8,128)(2,1)S(1)}, u32[]{:S(2)}, u32[]{:S(2)}) collective-permute-start(bf16[1,16,128]{2,1,0:T(8,128)(2,1)S(1)} %get-tuple-element.44), channel_id=1, source_target_pairs={{0,2},{2,4},{4,6},{6,8},{8,10},{10,12},{12,14},{14,16},{16,18},{18... | collective-permute-start | bytes 12296 | tf_op jit(solution)/shard_map/ppermute | solution.py:18
  146.8 4.1 %collective-permute-start.5 = (bf16[1,16,128]{2,1,0:T(8,128)(2,1)S(1)}, bf16[1,16,128]{2,1,0:T(8,128)(2,1)S(1)}, u32[]{:S(2)}, u32[]{:S(2)}) collective-permute-start(bf16[1,16,128]{2,1,0:T(8,128)(2,1)S(1)} %get-tuple-element.45), channel_id=1, source_target_pairs={{2,0},{4,2},{6,4},{8,6},{10,8},{12,10},{14,12},{16,14},{18,16},{20... | collective-permute-start | bytes 12296 | tf_op jit(solution)/shard_map/ppermute | solution.py:20
  151.1 0.6 collective-permute-done.5
  151.7 1.3 collective-permute-start.6
  153.0 3.2 %collective-permute-start.7 = (bf16[6,1,128]{2,1,0:T(2,128)(2,1)S(1)}, bf16[6,1,128]{2,1,0:T(2,128)(2,1)S(1)}, u32[]{:S(2)}, u32[]{:S(2)}) collective-permute-start(bf16[6,1,128]{2,1,0:T(2,128)(2,1)S(1)} %get-tuple-element.37), channel_id=1, source_target_pairs={{1,0},{3,2},{5,4},{7,6},{9,8},{11,10},{13,12},{15,14},{17,16},{19,... | collective-permute-start | bytes 4616 | tf_op jit(solution)/shard_map/ppermute | solution.py:20
  156.4 0.5 collective-permute-done.7
  157.7 0.8 fusion.28
  (57 shorter events, 2.8 us)
Async XLA Ops:
  0.6 84.1 %copy-start = (f32[1,256,128]{2,1,0:T(8,128)S(1)}, f32[1,256,128]{2,1,0:T(8,128)}, u32[]{:S(2)}) copy-start(f32[1,256,128]{2,1,0:T(8,128)} %param.18) | copy-start | bytes 393220
  1.3 8.5 %copy-start.5 = (f32[1,256]{1,0:T(1,128)S(1)}, f32[1,256]{1,0:T(1,128)}, u32[]{:S(2)}) copy-start(f32[1,256]{1,0:T(1,128)} %param.17) | copy-start | bytes 3076
  1.3 8.5 %copy-start.6 = (f32[1,256]{1,0:T(1,128)S(1)}, f32[1,256]{1,0:T(1,128)}, u32[]{:S(2)}) copy-start(f32[1,256]{1,0:T(1,128)} %param.20) | copy-start | bytes 3076
  3.4 21.2 %copy-start.4 = (s32[1,64,16]{1,2,0:T(8,128)S(1)}, s32[1,64,16]{1,2,0:T(8,128)}, u32[]{:S(2)}) copy-start(s32[1,64,16]{1,2,0:T(8,128)} %param.15) | copy-start | bytes 12292
  7.9 1.9 %copy-start.1 = (f32[64,16,4,256]{3,1,2,0:T(8,128)}, f32[64,16,4,256]{3,1,2,0:T(8,128)S(1)}, u32[]{:S(2)}) copy-start(f32[64,16,4,256]{3,1,2,0:T(8,128)S(1)} %fusion.2) | copy-start | bytes 12582916
  7.9 76.8 %copy-start.7 = (f32[1,128]{1,0:T(1,128)S(1)}, f32[1,128]{1,0:T(1,128)}, u32[]{:S(2)}) copy-start(f32[1,128]{1,0:T(1,128)} %param.19) | copy-start | bytes 1540
  90.0 30.2 %copy-start.2 = (bf16[3,3,128,128]{3,2,1,0:T(8,128)(2,1)S(1)}, bf16[3,3,128,128]{3,2,1,0:T(8,128)(2,1)}, u32[]{:S(2)}) copy-start(bf16[3,3,128,128]{3,2,1,0:T(8,128)(2,1)} %param.22) | copy-start | bytes 884740
  90.0 53.1 %copy-start.8 = (f32[128]{0:T(128)S(1)}, f32[128]{0:T(128)}, u32[]{:S(2)}) copy-start(f32[128]{0:T(128)} %param.23) | copy-start | bytes 1540
  90.0 60.9 %copy-start.3 = (bf16[3,3,128,128]{3,2,1,0:T(8,128)(2,1)S(1)}, bf16[3,3,128,128]{3,2,1,0:T(8,128)(2,1)}, u32[]{:S(2)}) copy-start(bf16[3,3,128,128]{3,2,1,0:T(8,128)(2,1)} %param.24) | copy-start | bytes 884740
  90.0 67.6 %copy-start.9 = (f32[128]{0:T(128)S(1)}, f32[128]{0:T(128)}, u32[]{:S(2)}) copy-start(f32[128]{0:T(128)} %param.25) | copy-start | bytes 1540
  113.1 7.2 %collective-permute-start = (bf16[1,16,128]{2,1,0:T(8,128)(2,1)S(1)}, bf16[1,16,128]{2,1,0:T(8,128)(2,1)S(1)}, u32[]{:S(2)}, u32[]{:S(2)}) collective-permute-start(bf16[1,16,128]{2,1,0:T(8,128)(2,1)S(1)} %get-tuple-element.46), channel_id=1, source_target_pairs={{0,2},{2,4},{4,6},{6,8},{8,10},{10,12},{12,14},{14,16},{16,18},{18... | collective-permute-start | bytes 12296 | tf_op jit(solution)/shard_map/ppermute | solution.py:18
  115.3 5.6 %collective-permute-start.1 = (bf16[1,16,128]{2,1,0:T(8,128)(2,1)S(1)}, bf16[1,16,128]{2,1,0:T(8,128)(2,1)S(1)}, u32[]{:S(2)}, u32[]{:S(2)}) collective-permute-start(bf16[1,16,128]{2,1,0:T(8,128)(2,1)S(1)} %get-tuple-element.47), channel_id=1, source_target_pairs={{2,0},{4,2},{6,4},{8,6},{10,8},{12,10},{14,12},{16,14},{18,16},{20... | collective-permute-start | bytes 12296 | tf_op jit(solution)/shard_map/ppermute | solution.py:20
  121.0 20.9 %collective-permute-start.2 = (bf16[6,1,128]{2,1,0:T(2,128)(2,1)S(1)}, bf16[6,1,128]{2,1,0:T(2,128)(2,1)S(1)}, u32[]{:S(2)}, u32[]{:S(2)}) collective-permute-start(bf16[6,1,128]{2,1,0:T(2,128)(2,1)S(1)} %get-tuple-element.40), channel_id=1, source_target_pairs={{0,1},{2,3},{4,5},{6,7},{8,9},{10,11},{12,13},{14,15},{16,17},{18,... | collective-permute-start | bytes 4616 | tf_op jit(solution)/shard_map/ppermute | solution.py:18
  122.3 20.2 %collective-permute-start.3 = (bf16[6,1,128]{2,1,0:T(2,128)(2,1)S(1)}, bf16[6,1,128]{2,1,0:T(2,128)(2,1)S(1)}, u32[]{:S(2)}, u32[]{:S(2)}) collective-permute-start(bf16[6,1,128]{2,1,0:T(2,128)(2,1)S(1)} %get-tuple-element.41), channel_id=1, source_target_pairs={{1,0},{3,2},{5,4},{7,6},{9,8},{11,10},{13,12},{15,14},{17,16},{19,... | collective-permute-start | bytes 4616 | tf_op jit(solution)/shard_map/ppermute | solution.py:20
  143.3 7.8 %collective-permute-start.4 = (bf16[1,16,128]{2,1,0:T(8,128)(2,1)S(1)}, bf16[1,16,128]{2,1,0:T(8,128)(2,1)S(1)}, u32[]{:S(2)}, u32[]{:S(2)}) collective-permute-start(bf16[1,16,128]{2,1,0:T(8,128)(2,1)S(1)} %get-tuple-element.44), channel_id=1, source_target_pairs={{0,2},{2,4},{4,6},{6,8},{8,10},{10,12},{12,14},{14,16},{16,18},{18... | collective-permute-start | bytes 12296 | tf_op jit(solution)/shard_map/ppermute | solution.py:18
  146.8 4.9 %collective-permute-start.5 = (bf16[1,16,128]{2,1,0:T(8,128)(2,1)S(1)}, bf16[1,16,128]{2,1,0:T(8,128)(2,1)S(1)}, u32[]{:S(2)}, u32[]{:S(2)}) collective-permute-start(bf16[1,16,128]{2,1,0:T(8,128)(2,1)S(1)} %get-tuple-element.45), channel_id=1, source_target_pairs={{2,0},{4,2},{6,4},{8,6},{10,8},{12,10},{14,12},{16,14},{18,16},{20... | collective-permute-start | bytes 12296 | tf_op jit(solution)/shard_map/ppermute | solution.py:20
  151.7 4.7 %collective-permute-start.6 = (bf16[6,1,128]{2,1,0:T(2,128)(2,1)S(1)}, bf16[6,1,128]{2,1,0:T(2,128)(2,1)S(1)}, u32[]{:S(2)}, u32[]{:S(2)}) collective-permute-start(bf16[6,1,128]{2,1,0:T(2,128)(2,1)S(1)} %get-tuple-element.36), channel_id=1, source_target_pairs={{0,1},{2,3},{4,5},{6,7},{8,9},{10,11},{12,13},{14,15},{16,17},{18,... | collective-permute-start | bytes 4616 | tf_op jit(solution)/shard_map/ppermute | solution.py:18
  153.0 4.0 %collective-permute-start.7 = (bf16[6,1,128]{2,1,0:T(2,128)(2,1)S(1)}, bf16[6,1,128]{2,1,0:T(2,128)(2,1)S(1)}, u32[]{:S(2)}, u32[]{:S(2)}) collective-permute-start(bf16[6,1,128]{2,1,0:T(2,128)(2,1)S(1)} %get-tuple-element.37), channel_id=1, source_target_pairs={{1,0},{3,2},{5,4},{7,6},{9,8},{11,10},{13,12},{15,14},{17,16},{19,... | collective-permute-start | bytes 4616 | tf_op jit(solution)/shard_map/ppermute | solution.py:20
where the time goes:
time: 160 us; the launch traced here: 158 us
  blocking collectives  74.3 us (46%)
  starting transfers between devices  39.8 us (25%)
  matrix products  34.7 us (22%)
  local copies, waits for them, and re-layouts  4.75 us (3%)
  waiting for transfers between devices  2.28 us (1%)
  between operations  1.63 us (1%)
    ppermute x4, starting transfers between devices, padded_2(): lax.ppermute(head, axis, [((i + 1) % count, i) for i in range(ends)])  31.5 us
    all_gather x1, blocking collectives, prefix_2(): gathered = lax.all_gather(part, axis)  29.8 us
    psum x1, blocking collectives, body(): total = lax.psum(depth, 'slab')  28.9 us
    all_to_all x1, blocking collectives, body(): lax.all_to_all(as_sent(blocked), 'slab', split_axis=0, concat_axis=0, til...  15.7 us
    dot_general x1, matrix products, densities(): jnp.einsum('rwkh,h->rwk', hidden_act, w_density, precision=lax.Precision....  14.7 us
    ppermute x4, starting transfers between devices, padded_2(): lax.ppermute(tail, axis, [(i, (i + 1) % count) for i in range(ends)])  8.28 us
    dot_general x1, matrix products, partial_image(): jnp.einsum('rwk,rwkc->rwc', weight, color, precision=lax.Precision.HIGHEST)  7.32 us
    dot_general x1, matrix products, partial_image(): jnp.einsum('rwkh,hc->rwkc', hidden_act, w_color, precision=lax.Precision....  5.27 us
  transfers between devices with their start and end apart: 8, of which 4 were waited for; matrix products, arithmetic and copies ran while one was open for 0% of the time, Pallas kernels for 0%

commit v1 on v0

v1 whole, which is shorter than its diff:
```python
import functools

import jax
import jax.numpy as jnp
from jax import lax
from jax.experimental import pallas as pl
from jax.experimental.pallas import tpu as pltpu
from jax.sharding import PartitionSpec as P

F = 64
K = 4
LANES = 128
MESH = pl.DeviceIdType.MESH
BF16 = jnp.bfloat16
F32 = jnp.float32


def dot(a, b):
    return jnp.dot(a, b, preferred_element_type=F32)


def render_kernel(
    slabs,
    samples_hbm,
    counts_ref,
    w_in_hbm,
    b_in_ref,
    w_color_hbm,
    b_color_ref,
    w_density_ref,
    b_density_ref,
    conv_a_hbm,
    bias_a_ref,
    conv_b_hbm,
    bias_b_ref,
    decoded_ref,
    front_ref,
    samples_ref,
    w_in_ref,
    w_color_ref,
    conv_a_ref,
    conv_b_ref,
    taps_a,
    taps_b,
    density_ref,
    colors_ref,
    weight_ref,
    depths_ref,
    sent_ref,
    parts_ref,
    field_ref,
    load_sems,
    depth_send,
    depth_recv,
    part_send,
    part_recv,
    edge_send,
    edge_recv,
):
    me = lax.axis_index("slab")
    tile = lax.axis_index("tile")
    other = 1 - tile
    rows, cols = samples_ref.shape[0], samples_ref.shape[1]
    groups = rows * cols // LANES
    group_rows = LANES // cols
    strip = rows // slabs
    strip_rays = strip * cols
    hid = w_in_ref.shape[1]
    channels = w_color_ref.shape[1]
    not_first = me > 0
    not_last = me < slabs - 1

    loads = [
        pltpu.make_async_copy(src, dst, load_sems.at[i])
        for i, (src, dst) in enumerate(
            (
                (w_in_hbm.at[0], w_in_ref),
                (samples_hbm.at[0], samples_ref),
                (w_color_hbm.at[0], w_color_ref),
                (conv_a_hbm, conv_a_ref),
                (conv_b_hbm, conv_b_ref),
            )
        )
    ]
    for load in loads:
        load.start()

    barrier = pltpu.get_barrier_semaphore()

    def greet(slab, tile_at):
        pl.semaphore_signal(barrier, inc=1, device_id=(slab, tile_at), device_id_type=MESH)

    def greet_slab(shift, carry):
        greet(lax.rem(me + shift, slabs), tile)
        return carry

    lax.fori_loop(1, slabs, greet_slab, 0)
    greet(me, other)

    @pl.when(not_first)
    def _():
        greet(me - 1, other)

    @pl.when(not_last)
    def _():
        greet(me + 1, other)

    eye = lax.broadcasted_iota(jnp.int32, (LANES, LANES), 0) == lax.broadcasted_iota(
        jnp.int32, (LANES, LANES), 1
    )

    loads[0].wait()
    w_in = w_in_ref[...]
    high = w_in.astype(BF16)
    low = (w_in - high.astype(F32)).astype(BF16)
    blank = jnp.zeros_like(high)
    even = [high, blank, high, blank, low, blank]
    odd = [blank, high, blank, high, blank, low]
    pair_w = jnp.concatenate(
        [jnp.concatenate(even, axis=0), jnp.concatenate(odd, axis=0)], axis=1
    )
    pair_b = jnp.concatenate([b_in_ref[...], b_in_ref[...]], axis=1)
    loads[2].wait()
    density_cols = jnp.transpose(jnp.broadcast_to(w_density_ref[...], (LANES, hid)))
    heads = jnp.concatenate([w_color_ref[...].astype(BF16), density_cols.astype(BF16)], axis=1)
    b_color = b_color_ref[...]
    loads[1].wait()
    chunk = 2
    for c in range(groups // chunk):
        rays = chunk * LANES
        x = samples_ref[c * chunk * group_rows : (c + 1) * chunk * group_rows].reshape(rays, K * F)
        for pair in range(K // 2):
            part = x[:, pair * LANES : (pair + 1) * LANES]
            part_high = part.astype(BF16)
            part_low = (part - part_high.astype(F32)).astype(BF16)
            both = jnp.concatenate([part_high, part_low, part_high], axis=1)
            act = jnp.maximum(dot(both, pair_w) + pair_b, 0.0).astype(BF16)
            for half in range(2):
                k = 2 * pair + half
                out = dot(act[:, half * hid : (half + 1) * hid], heads)
                color = (out[:, :channels] + b_color).astype(BF16)
                before = out[:, channels:].reshape(chunk, LANES, LANES)
                for g in range(chunk):
                    colors_ref[c * chunk + g, k * LANES : (k + 1) * LANES, :] = color[
                        g * LANES : (g + 1) * LANES
                    ]
                density_ref[k, c * chunk : (c + 1) * chunk, :] = jnp.sum(
                    jnp.where(eye, before, 0.0), axis=1
                )

    spread = (
        lax.rem(lax.broadcasted_iota(jnp.int32, (cols, LANES), 1), cols)
        == lax.broadcasted_iota(jnp.int32, (cols, LANES), 0)
    ).astype(BF16)
    own_lane = (
        lax.broadcasted_iota(jnp.int32, (group_rows, LANES), 1) // cols
        == lax.broadcasted_iota(jnp.int32, (group_rows, LANES), 0)
    )
    live = dot(counts_ref[0].astype(F32).astype(BF16), spread).reshape(groups, group_rows, LANES)
    live = jnp.sum(jnp.where(own_lane, live, 0.0), axis=1)

    density = []
    for k in range(K):
        z = density_ref[k] + b_density_ref[0]
        soft = jnp.maximum(z, 0.0) + jnp.log1p(jnp.exp(-jnp.abs(z)))
        density.append(jnp.where(live > k, soft, 0.0))
    depths_ref[me] = density[0] + density[1] + density[2] + density[3]

    pl.semaphore_wait(
        barrier, slabs + not_first.astype(jnp.int32) + not_last.astype(jnp.int32)
    )

    def send_depth(shift, carry):
        pltpu.make_async_remote_copy(
            src_ref=depths_ref.at[me],
            dst_ref=depths_ref.at[me],
            send_sem=depth_send,
            recv_sem=depth_recv,
            device_id=(lax.rem(me + shift, slabs), tile),
            device_id_type=MESH,
        ).start()
        return carry

    lax.fori_loop(1, slabs, send_depth, 0)

    loads[3].wait()
    loads[4].wait()
    for taps, conv in ((taps_a, conv_a_ref), (taps_b, conv_b_ref)):
        for r in range(3):
            for s in range(3):
                taps[r * channels : (r + 1) * channels, s * channels : (s + 1) * channels] = conv[
                    r, s
                ]

    peers = depths_ref.at[pl.ds(0, slabs - 1)]
    pltpu.make_async_copy(peers, peers, depth_recv).wait()
    total = depths_ref[0]
    prefix = jnp.where(me > 0, depths_ref[0], 0.0)
    for s in range(1, slabs):
        one = depths_ref[s]
        total = total + one
        prefix = prefix + jnp.where(s < me, one, 0.0)
    front = prefix / total
    ahead = front
    for k in range(K):
        scaled = density[k] / total
        weight_ref[k] = jnp.exp(-ahead) * (1.0 - jnp.exp(-scaled))
        ahead = ahead + scaled

    def send_part(owner):
        pltpu.make_async_remote_copy(
            src_ref=sent_ref.at[owner],
            dst_ref=parts_ref.at[me],
            send_sem=part_send,
            recv_sem=part_recv,
            device_id=(owner, tile),
            device_id_type=MESH,
        ).start()

    strips = LANES // strip_rays
    place = lax.rem(me, strips)
    for i in range(groups):
        g = lax.rem(me // strips + i, groups)
        diag = [
            jnp.where(eye, weight_ref[k, pl.ds(g, 1), :], 0.0).astype(BF16) for k in range(K)
        ]
        image = dot(jnp.concatenate(diag, axis=1), colors_ref[g]).astype(BF16)
        sent_ref[pl.ds(strips * g, strips)] = image.reshape(strips, strip_rays, channels)
        for j in range(strips):
            if i > 0:
                send_part(strips * g + j)
            elif j > 0:
                send_part(strips * g + lax.rem(place + j, strips))
    parts_ref[me] = sent_ref[me]

    laid = jnp.where(own_lane, front[:, None, :], 0.0).reshape(rows, LANES)
    gather = (
        lax.rem(lax.broadcasted_iota(jnp.int32, (LANES, cols), 0), cols)
        == lax.broadcasted_iota(jnp.int32, (LANES, cols), 1)
    ).astype(BF16)
    first = laid.astype(BF16)
    rest = laid - first.astype(F32)
    second = rest.astype(BF16)
    third = (rest - second.astype(F32)).astype(BF16)
    front_ref[0] = dot(first, gather) + dot(second, gather) + dot(third, gather)

    peers = parts_ref.at[pl.ds(0, slabs - 1)]
    pltpu.make_async_copy(peers, peers, part_recv).wait()
    image = parts_ref[0].astype(F32)
    for s in range(1, slabs):
        image = image + parts_ref[s].astype(F32)
    image = image.astype(BF16).reshape(strip, cols, channels)

    field_ref[0, 2 : 2 + strip] = image
    edge = jnp.zeros((2, 2, cols, channels), BF16)

    def edge_copy(which, source, target, device):
        return pltpu.make_async_remote_copy(
            src_ref=source,
            dst_ref=target,
            send_sem=edge_send.at[which],
            recv_sem=edge_recv.at[which],
            device_id=device,
            device_id_type=MESH,
        )

    own = field_ref.at[0, pl.ds(2, strip)]
    head = field_ref.at[0, pl.ds(2, 2)]
    tail = field_ref.at[0, pl.ds(strip, 2)]
    up = [
        edge_copy(1, head, field_ref.at[0, pl.ds(strip + 2, 2)], (me - 1, tile)),
        edge_copy(2, head, field_ref.at[1, pl.ds(strip + 2, 2)], (me - 1, other)),
    ]
    down = [
        edge_copy(3, tail, field_ref.at[0, pl.ds(0, 2)], (me + 1, tile)),
        edge_copy(4, tail, field_ref.at[1, pl.ds(0, 2)], (me + 1, other)),
    ]
    across = edge_copy(0, own, field_ref.at[1, pl.ds(2, strip)], (me, other))

    @pl.when(not_first)
    def _():
        for copy in up:
            copy.start()

    @pl.when(not_last)
    def _():
        for copy in down:
            copy.start()

    across.start()

    @pl.when(jnp.logical_not(not_first))
    def _():
        field_ref[:, 0:2] = edge

    @pl.when(jnp.logical_not(not_last))
    def _():
        field_ref[:, strip + 2 : strip + 4] = edge

    @pl.when(not_last)
    def _():
        for copy in up:
            copy.wait_recv()

    @pl.when(not_first)
    def _():
        for copy in down:
            copy.wait_recv()

    across.wait_recv()

    place = lax.broadcasted_iota(jnp.int32, (1, cols, 1), 1)
    near = jnp.where(tile == 0, place, cols - 1 - place) < 2
    side = jnp.where(near, field_ref[1].astype(F32), 0.0).astype(BF16)
    ring = jnp.concatenate([field_ref[0], side], axis=1)

    def convolve(cells, taps, bias):
        out_rows = cells.shape[0] - 2
        span = cells.shape[1]
        stacked = jnp.concatenate(
            [cells[r : r + out_rows].reshape(out_rows * span, channels) for r in range(3)], axis=1
        )
        shifted = dot(stacked, taps[...]).reshape(out_rows, span, 3 * channels)
        return (
            pltpu.roll(shifted[:, :, :channels], 1, 1)
            + shifted[:, :, channels : 2 * channels]
            + pltpu.roll(shifted[:, :, 2 * channels :], span - 1, 1)
            + bias
        )

    hidden_map = jnp.maximum(convolve(ring, taps_a, bias_a_ref[...].reshape(1, 1, channels)), 0.0)
    shape = (strip + 2, 2 * cols, 1)
    at_row = lax.broadcasted_iota(jnp.int32, shape, 0) + me * strip - 1
    at_col = lax.broadcasted_iota(jnp.int32, shape, 1)
    in_rows = jnp.logical_and(at_row >= 0, at_row < rows)
    outside = jnp.where(tile == 0, 2 * cols - 1, cols)
    hidden_map = jnp.where(jnp.logical_and(in_rows, at_col != outside), hidden_map, 0.0)
    decoded = convolve(hidden_map.astype(BF16), taps_b, bias_b_ref[...].reshape(1, 1, channels))
    decoded_ref[...] = decoded[:, :cols].astype(BF16)

    peers = depths_ref.at[pl.ds(0, slabs - 1)]
    pltpu.make_async_copy(peers, peers, depth_send).wait()
    peers = parts_ref.at[pl.ds(0, slabs - 1)]
    pltpu.make_async_copy(peers, peers, part_send).wait()
    across.wait_send()

    @pl.when(not_first)
    def _():
        for copy in up:
            copy.wait_send()

    @pl.when(not_last)
    def _():
        for copy in down:
            copy.wait_send()


def body(
    slabs,
    samples,
    counts,
    w_in,
    b_in,
    w_color,
    b_color,
    w_density,
    b_density,
    conv_a,
    bias_a,
    conv_b,
    bias_b,
):
    _, rows, cols, width = samples.shape
    hid, channels = w_color.shape[1:]
    groups = rows * cols // LANES
    strip = rows // slabs
    vmem = pl.BlockSpec(memory_space=pltpu.VMEM)
    smem = pl.BlockSpec(memory_space=pltpu.SMEM)
    hbm = pl.BlockSpec(memory_space=pl.ANY)
    dma = pltpu.SemaphoreType.DMA
    return pl.pallas_call(
        functools.partial(render_kernel, slabs),
        out_shape=(
            jax.ShapeDtypeStruct((strip, cols, channels), BF16),
            jax.ShapeDtypeStruct((1, rows, cols), F32),
        ),
        in_specs=[hbm, vmem, hbm, vmem, hbm, vmem, vmem, smem, hbm, vmem, hbm, vmem],
        out_specs=(vmem, vmem),
        scratch_shapes=[
            pltpu.VMEM((rows, cols, width), F32),
            pltpu.VMEM(w_in.shape[1:], F32),
            pltpu.VMEM(w_color.shape[1:], F32),
            pltpu.VMEM(conv_a.shape, BF16),
            pltpu.VMEM(conv_b.shape, BF16),
            pltpu.VMEM((3 * channels, 3 * channels), BF16),
            pltpu.VMEM((3 * channels, 3 * channels), BF16),
            pltpu.VMEM((K, groups, LANES), F32),
            pltpu.VMEM((groups, K * LANES, channels), BF16),
            pltpu.VMEM((K, groups, LANES), F32),
            pltpu.VMEM((slabs, groups, LANES), F32),
            pltpu.VMEM((slabs, strip * cols, channels), BF16),
            pltpu.VMEM((slabs, strip * cols, channels), BF16),
            pltpu.VMEM((2, strip + 4, cols, channels), BF16),
            dma((5,)),
            dma,
            dma,
            dma,
            dma,
            dma((5,)),
            dma((5,)),
        ],
        compiler_params=pltpu.CompilerParams(
            collective_id=0, has_side_effects=True, vmem_limit_bytes=40 * 2**20
        ),
    )(
        samples,
        counts,
        w_in,
        b_in,
        w_color,
        b_color,
        w_density,
        b_density,
        conv_a,
        bias_a.reshape(1, channels),
        conv_b,
        bias_b.reshape(1, channels),
    )


def solution(mesh):
    in_specs = (
        P("slab", None, "tile", None),
        P("slab", None, "tile"),
        P("slab", None, None),
        P("slab", None),
        P("slab", None, None),
        P("slab", None),
        P("slab", None),
        P("slab"),
        P(),
        P(),
        P(),
        P(),
    )
    out_specs = (P("slab", "tile", None), P("slab", None, "tile"))
    run = functools.partial(body, mesh.shape["slab"])
    return jax.shard_map(run, mesh=mesh, in_specs=in_specs, out_specs=out_specs, check_vma=False)
```

time: 160 us -> 30.3 us (0.19)
  the two profiles are of different devices: /device:TPU:9 before, /device:TPU:17 now
where the time goes in v1:
time: 30.3 us; the launch traced here: 30 us
  Pallas kernels  21.6 us (71%)
  local copies, waits for them, and re-layouts  6.99 us (23%)
  between operations  1.37 us (5%)
    pallas_call x1, Pallas kernels, body(): pl.pallas_call(functools.partial(render_kernel, slabs), out_shape=(jax.Sh...  21.6 us
    unnamed x22, local copies, waits for them, and re-layouts  6.32 us
    pallas_call x1, local copies, waits for them, and re-layouts, body(): pl.pallas_call(functools.partial(render_kernel, slabs), out_shape=(jax.Sh...  0.67 us

profile of v1, /device:TPU:17, one launch (start us, length us, event | category | flops | bytes accessed | tf_op | source)
XLA Modules:
  0.0 30.0 jit_solution(891256944421923422)
XLA Ops:
  1.3 0.0 copy-start.5
  1.3 0.0 copy-start.6
  1.3 0.0 copy-start.7
  1.3 0.0 copy-start.8
  1.3 0.0 copy-start.9
  1.3 0.8 %copy.14.counts_ref = s32[1,64,16]{2,1,0:T(8,128)S(1)} copy(s32[1,64,16]{1,2,0:T(8,128)} %param.13) | data formatting | bytes 8192 | tf_op args[1]
  2.1 0.0 copy-done.5
  2.1 0.0 copy-done.6
  2.1 0.0 copy-done.7
  2.2 0.0 copy-done.8
  2.2 0.0 copy-done.9
  2.2 0.0 copy-start
  2.2 1.2 %copy-done = f32[1,64,16,256]{3,2,1,0:T(8,128)S(1)} copy-done((f32[1,64,16,256]{3,2,1,0:T(8,128)S(1)}, f32[1,64,16,256]{3,2,1,0:T(8,128)}, u32[]{:S(2)}) %copy-start) | copy-done | bytes 1048600
  3.4 0.0 copy-start.1
  3.4 1.0 %copy-done.1 = bf16[3,3,128,128]{3,2,1,0:T(8,128)(2,1)S(1)} copy-done((bf16[3,3,128,128]{3,2,1,0:T(8,128)(2,1)S(1)}, bf16[3,3,128,128]{3,2,1,0:T(8,128)(2,1)}, u32[]{:S(2)}) %copy-start.1) | copy-done | bytes 294936
  4.4 0.0 copy-start.2
  4.4 1.0 %copy-done.2 = bf16[3,3,128,128]{3,2,1,0:T(8,128)(2,1)S(1)} copy-done((bf16[3,3,128,128]{3,2,1,0:T(8,128)(2,1)S(1)}, bf16[3,3,128,128]{3,2,1,0:T(8,128)(2,1)}, u32[]{:S(2)}) %copy-start.2) | copy-done | bytes 294936
  5.3 0.0 copy-start.3
  5.3 0.9 %copy-done.3 = f32[1,256,128]{2,1,0:T(8,128)S(1)} copy-done((f32[1,256,128]{2,1,0:T(8,128)S(1)}, f32[1,256,128]{2,1,0:T(8,128)}, u32[]{:S(2)}) %copy-start.3) | copy-done | bytes 131096
  6.2 0.0 copy-start.4
  6.2 0.8 %copy-done.4 = f32[1,64,256]{2,1,0:T(8,128)S(1)} copy-done((f32[1,64,256]{2,1,0:T(8,128)S(1)}, f32[1,64,256]{2,1,0:T(8,128)}, u32[]{:S(2)}) %copy-start.4) | copy-done | bytes 65560
  7.1 21.6 %shard_map.131 = (bf16[4,16,128]{2,1,0:T(8,128)(2,1)S(1)}, f32[1,64,16]{2,1,0:T(8,128)S(1)}) custom-call(f32[1,64,16,256]{3,2,1,0:T(8,128)S(1)} %copy-done, s32[1,64,16]{2,1,0:T(8,128)S(1)} %copy.14.counts_ref, f32[1,64,256]{2,1,0:T(8,128)S(1)} %copy-done.4, f32[1,256]{1,0:T(1,128)S(1)} %copy-done.5, f32[1,256,128]{2,1,0:T(8,128)S(1)} %copy-done.3, ...), custom_call_target="tpu_custom_call" | custom-call | tf_op jit(solution)/shard_map/pallas_call | solution.py:381
  28.7 0.7 %copy.15 = f32[1,64,16]{1,2,0:T(8,128)} copy(f32[1,64,16]{2,1,0:T(8,128)S(1)} %get-tuple-element.3) | data formatting | bytes 8192 | tf_op jit(solution)/shard_map/pallas_call | solution.py:381
  29.4 0.6 %copy.18 = bf16[4,16,128]{2,1,0:T(8,128)(2,1)} copy(bf16[4,16,128]{2,1,0:T(8,128)(2,1)S(1)} %get-tuple-element.6) | data formatting | bytes 32768
Async XLA Ops:
  1.3 0.9 %copy-start.5 = (f32[1,256]{1,0:T(1,128)S(1)}, f32[1,256]{1,0:T(1,128)}, u32[]{:S(2)}) copy-start(f32[1,256]{1,0:T(1,128)} %b_in_ref.1) | copy-start | bytes 3076
  1.3 0.9 %copy-start.6 = (f32[1,256]{1,0:T(1,128)S(1)}, f32[1,256]{1,0:T(1,128)}, u32[]{:S(2)}) copy-start(f32[1,256]{1,0:T(1,128)} %w_density_ref.1) | copy-start | bytes 3076
  1.3 0.9 %copy-start.7 = (f32[1,128]{1,0:T(1,128)S(1)}, f32[1,128]{1,0:T(1,128)}, u32[]{:S(2)}) copy-start(f32[1,128]{1,0:T(1,128)} %b_color_ref.1) | copy-start | bytes 1540
  1.3 0.9 %copy-start.8 = (f32[128]{0:T(128)S(1)}, f32[128]{0:T(128)}, u32[]{:S(2)}) copy-start(f32[128]{0:T(128)} %param.21) | copy-start | bytes 1540
  1.3 0.9 %copy-start.9 = (f32[128]{0:T(128)S(1)}, f32[128]{0:T(128)}, u32[]{:S(2)}) copy-start(f32[128]{0:T(128)} %param.23) | copy-start | bytes 1540
  2.2 1.2 %copy-start = (f32[1,64,16,256]{3,2,1,0:T(8,128)S(1)}, f32[1,64,16,256]{3,2,1,0:T(8,128)}, u32[]{:S(2)}) copy-start(f32[1,64,16,256]{3,2,1,0:T(8,128)} %samples_hbm.1) | copy-start | bytes 3145732
  3.4 1.0 %copy-start.1 = (bf16[3,3,128,128]{3,2,1,0:T(8,128)(2,1)S(1)}, bf16[3,3,128,128]{3,2,1,0:T(8,128)(2,1)}, u32[]{:S(2)}) copy-start(bf16[3,3,128,128]{3,2,1,0:T(8,128)(2,1)} %conv_a_hbm.1) | copy-start | bytes 884740
  4.4 1.0 %copy-start.2 = (bf16[3,3,128,128]{3,2,1,0:T(8,128)(2,1)S(1)}, bf16[3,3,128,128]{3,2,1,0:T(8,128)(2,1)}, u32[]{:S(2)}) copy-start(bf16[3,3,128,128]{3,2,1,0:T(8,128)(2,1)} %conv_b_hbm.1) | copy-start | bytes 884740
  5.3 0.9 %copy-start.3 = (f32[1,256,128]{2,1,0:T(8,128)S(1)}, f32[1,256,128]{2,1,0:T(8,128)}, u32[]{:S(2)}) copy-start(f32[1,256,128]{2,1,0:T(8,128)} %w_color_hbm.1) | copy-start | bytes 393220
  6.2 0.8 %copy-start.4 = (f32[1,64,256]{2,1,0:T(8,128)S(1)}, f32[1,64,256]{2,1,0:T(8,128)}, u32[]{:S(2)}) copy-start(f32[1,64,256]{2,1,0:T(8,128)} %w_in_hbm.1) | copy-start | bytes 196612

commit v2 on v1

--- a/solution.py
+++ b/solution.py
@@ -19,27 +19,37 @@
     return jnp.dot(a, b, preferred_element_type=F32)
 
 
+def dot_last(a, b):
+    return lax.dot_general(a, b, (((1,), (1,)), ((), ())), preferred_element_type=F32)
+
+
 def render_kernel(
     slabs,
     samples_hbm,
-    counts_ref,
+    counts_hbm,
     w_in_hbm,
-    b_in_ref,
+    b_in_hbm,
     w_color_hbm,
-    b_color_ref,
-    w_density_ref,
+    b_color_hbm,
+    w_density_hbm,
     b_density_ref,
     conv_a_hbm,
-    bias_a_ref,
+    bias_a_hbm,
     conv_b_hbm,
-    bias_b_ref,
+    bias_b_hbm,
     decoded_ref,
     front_ref,
     samples_ref,
+    counts_ref,
     w_in_ref,
+    b_in_ref,
     w_color_ref,
+    b_color_ref,
+    w_density_ref,
     conv_a_ref,
+    bias_a_ref,
     conv_b_ref,
+    bias_b_ref,
     taps_a,
     taps_b,
     density_ref,
@@ -70,19 +80,32 @@
     not_first = me > 0
     not_last = me < slabs - 1
 
+    chunk = 2
+    chunk_rows = chunk * group_rows
+    pieces = [pl.ds(i * chunk_rows, chunk_rows) for i in range(groups // chunk)]
+    first_loads = [
+        (w_in_hbm.at[0], w_in_ref),
+        (b_in_hbm, b_in_ref),
+        (w_color_hbm.at[0], w_color_ref),
+        (w_density_hbm, w_density_ref),
+        (b_color_hbm, b_color_ref),
+    ]
+    last_loads = [
+        (counts_hbm.at[0], counts_ref),
+        (conv_a_hbm, conv_a_ref),
+        (conv_b_hbm, conv_b_ref),
+        (bias_a_hbm, bias_a_ref),
+        (bias_b_hbm, bias_b_ref),
+    ]
+    sample_loads = [(samples_hbm.at[0, piece], samples_ref.at[piece]) for piece in pieces]
     loads = [
         pltpu.make_async_copy(src, dst, load_sems.at[i])
-        for i, (src, dst) in enumerate(
-            (
-                (w_in_hbm.at[0], w_in_ref),
-                (samples_hbm.at[0], samples_ref),
-                (w_color_hbm.at[0], w_color_ref),
-                (conv_a_hbm, conv_a_ref),
-                (conv_b_hbm, conv_b_ref),
-            )
-        )
+        for i, (src, dst) in enumerate(first_loads + last_loads + sample_loads)
     ]
-    for load in loads:
+    sample_loads = loads[len(first_loads) + len(last_loads) :]
+    last_loads = loads[len(first_loads) : len(first_loads) + len(last_loads)]
+    first_loads = loads[: len(first_loads)]
+    for load in first_loads + sample_loads + last_loads:
         load.start()
 
     barrier = pltpu.get_barrier_semaphore()
@@ -109,7 +132,8 @@
         jnp.int32, (LANES, LANES), 1
     )
 
-    loads[0].wait()
+    for load in first_loads:
+        load.wait()
     w_in = w_in_ref[...]
     high = w_in.astype(BF16)
     low = (w_in - high.astype(F32)).astype(BF16)
@@ -120,14 +144,12 @@
         [jnp.concatenate(even, axis=0), jnp.concatenate(odd, axis=0)], axis=1
     )
     pair_b = jnp.concatenate([b_in_ref[...], b_in_ref[...]], axis=1)
-    loads[2].wait()
     density_cols = jnp.transpose(jnp.broadcast_to(w_density_ref[...], (LANES, hid)))
     heads = jnp.concatenate([w_color_ref[...].astype(BF16), density_cols.astype(BF16)], axis=1)
     b_color = b_color_ref[...]
-    loads[1].wait()
-    chunk = 2
     for c in range(groups // chunk):
         rays = chunk * LANES
+        sample_loads[c].wait()
         x = samples_ref[c * chunk * group_rows : (c + 1) * chunk * group_rows].reshape(rays, K * F)
         for pair in range(K // 2):
             part = x[:, pair * LANES : (pair + 1) * LANES]
@@ -148,6 +170,9 @@
                     jnp.where(eye, before, 0.0), axis=1
                 )
 
+    for load in last_loads:
+        load.wait()
+
     spread = (
         lax.rem(lax.broadcasted_iota(jnp.int32, (cols, LANES), 1), cols)
         == lax.broadcasted_iota(jnp.int32, (cols, LANES), 0)
@@ -156,7 +181,12 @@
         lax.broadcasted_iota(jnp.int32, (group_rows, LANES), 1) // cols
         == lax.broadcasted_iota(jnp.int32, (group_rows, LANES), 0)
     )
-    live = dot(counts_ref[0].astype(F32).astype(BF16), spread).reshape(groups, group_rows, LANES)
+    row_eye = (
+        lax.broadcasted_iota(jnp.int32, (rows, rows), 0)
+        == lax.broadcasted_iota(jnp.int32, (rows, rows), 1)
+    ).astype(BF16)
+    by_row = dot_last(row_eye, counts_ref[...].astype(F32).astype(BF16)).astype(BF16)
+    live = dot(by_row, spread).reshape(groups, group_rows, LANES)
     live = jnp.sum(jnp.where(own_lane, live, 0.0), axis=1)
 
     density = []
@@ -183,8 +213,6 @@
 
     lax.fori_loop(1, slabs, send_depth, 0)
 
-    loads[3].wait()
-    loads[4].wait()
     for taps, conv in ((taps_a, conv_a_ref), (taps_b, conv_b_ref)):
         for r in range(3):
             for s in range(3):
@@ -234,15 +262,11 @@
     parts_ref[me] = sent_ref[me]
 
     laid = jnp.where(own_lane, front[:, None, :], 0.0).reshape(rows, LANES)
-    gather = (
-        lax.rem(lax.broadcasted_iota(jnp.int32, (LANES, cols), 0), cols)
-        == lax.broadcasted_iota(jnp.int32, (LANES, cols), 1)
-    ).astype(BF16)
     first = laid.astype(BF16)
     rest = laid - first.astype(F32)
     second = rest.astype(BF16)
     third = (rest - second.astype(F32)).astype(BF16)
-    front_ref[0] = dot(first, gather) + dot(second, gather) + dot(third, gather)
+    front_ref[0] = dot_last(spread, first) + dot_last(spread, second) + dot_last(spread, third)
 
     peers = parts_ref.at[pl.ds(0, slabs - 1)]
     pltpu.make_async_copy(peers, peers, part_recv).wait()
@@ -378,20 +402,27 @@
     smem = pl.BlockSpec(memory_space=pltpu.SMEM)
     hbm = pl.BlockSpec(memory_space=pl.ANY)
     dma = pltpu.SemaphoreType.DMA
-    return pl.pallas_call(
+    pieces = rows * cols // (2 * LANES)
+    decoded, front = pl.pallas_call(
         functools.partial(render_kernel, slabs),
         out_shape=(
             jax.ShapeDtypeStruct((strip, cols, channels), BF16),
-            jax.ShapeDtypeStruct((1, rows, cols), F32),
+            jax.ShapeDtypeStruct((1, cols, rows), F32),
         ),
-        in_specs=[hbm, vmem, hbm, vmem, hbm, vmem, vmem, smem, hbm, vmem, hbm, vmem],
+        in_specs=[hbm] * 7 + [smem] + [hbm] * 4,
         out_specs=(vmem, vmem),
         scratch_shapes=[
             pltpu.VMEM((rows, cols, width), F32),
+            pltpu.VMEM((cols, rows), jnp.int32),
             pltpu.VMEM(w_in.shape[1:], F32),
+            pltpu.VMEM((1, hid), F32),
             pltpu.VMEM(w_color.shape[1:], F32),
+            pltpu.VMEM((1, channels), F32),
+            pltpu.VMEM((1, hid), F32),
             pltpu.VMEM(conv_a.shape, BF16),
+            pltpu.VMEM((1, channels), F32),
             pltpu.VMEM(conv_b.shape, BF16),
+            pltpu.VMEM((1, channels), F32),
             pltpu.VMEM((3 * channels, 3 * channels), BF16),
             pltpu.VMEM((3 * channels, 3 * channels), BF16),
             pltpu.VMEM((K, groups, LANES), F32),
@@ -401,7 +432,7 @@
             pltpu.VMEM((slabs, strip * cols, channels), BF16),
             pltpu.VMEM((slabs, strip * cols, channels), BF16),
             pltpu.VMEM((2, strip + 4, cols, channels), BF16),
-            dma((5,)),
+            dma((10 + pieces,)),
             dma,
             dma,
             dma,
@@ -410,11 +441,11 @@
             dma((5,)),
         ],
         compiler_params=pltpu.CompilerParams(
-            collective_id=0, has_side_effects=True, vmem_limit_bytes=40 * 2**20
+            collective_id=0, has_side_effects=True, vmem_limit_bytes=60 * 2**20
         ),
     )(
         samples,
-        counts,
+        jnp.swapaxes(counts, 1, 2),
         w_in,
         b_in,
         w_color,
@@ -426,6 +457,7 @@
         conv_b,
         bias_b.reshape(1, channels),
     )
+    return decoded, jnp.swapaxes(front, 1, 2)
 
 
 def solution(mesh):

time: 30.3 us -> 26.5 us (0.87)
  the two profiles are of different devices: /device:TPU:17 before, /device:TPU:9 now
where the time goes in v2:
time: 26.5 us; the launch traced here: 26.2 us
  Pallas kernels  22.9 us (86%)
  local copies, waits for them, and re-layouts  1.93 us (7%)
  between operations  1.3 us (5%)
    pallas_call x1, Pallas kernels, body(): pl.pallas_call(functools.partial(render_kernel, slabs), out_shape=(jax.Sh...  22.9 us
    unnamed x4, local copies, waits for them, and re-layouts  1.93 us

profile of v2, /device:TPU:9, one launch (start us, length us, event | category | flops | bytes accessed | tf_op | source)
XLA Modules:
  0.0 26.2 jit_solution(10627247503318315050)
XLA Ops:
  1.3 22.9 %shard_map.131 = (bf16[4,16,128]{2,1,0:T(8,128)(2,1)}, f32[1,16,64]{2,1,0:T(8,128)}) custom-call(f32[1,64,16,256]{3,2,1,0:T(8,128)} %samples_hbm.1, s32[1,16,64]{2,1,0:T(8,128)} %bitcast.4, f32[1,64,256]{2,1,0:T(8,128)} %w_in_hbm.1, f32[1,256]{1,0:T(1,128)} %b_in_hbm.1, f32[1,256,128]{2,1,0:T(8,128)} %w_color_hbm.1, f32[1,128]{1,0:T(1,128)} %b_color_hbm.1, ...), custom_call_target="tpu_custom_call" | custom-call | tf_op jit(solution)/shard_map/pallas_call | solution.py:406
  24.2 0.0 copy-start
  24.2 1.3 %copy.17 = bf16[4,16,128]{2,1,0:T(8,128)(2,1)} copy(bf16[4,16,128]{2,1,0:T(8,128)(2,1)} %get-tuple-element.8) | data formatting | bytes 32768
  25.6 0.0 copy-done
  25.6 0.6 %copy.18 = f32[1,64,16]{1,2,0:T(8,128)} copy(f32[1,64,16]{1,2,0:T(8,128)S(1)} %bitcast.5) | data formatting | bytes 8192
Async XLA Ops:
  24.2 1.3 %copy-start = (f32[1,16,64]{2,1,0:T(8,128)S(1)}, f32[1,16,64]{2,1,0:T(8,128)}, u32[]{:S(2)}) copy-start(f32[1,16,64]{2,1,0:T(8,128)} %get-tuple-element.5) | copy-start | bytes 12292

commit v3 on v2

--- a/solution.py
+++ b/solution.py
@@ -10,6 +10,7 @@
 F = 64
 K = 4
 LANES = 128
+HALVES = 2
 MESH = pl.DeviceIdType.MESH
 BF16 = jnp.bfloat16
 F32 = jnp.float32
@@ -80,9 +81,9 @@
     not_first = me > 0
     not_last = me < slabs - 1
 
-    chunk = 2
-    chunk_rows = chunk * group_rows
-    pieces = [pl.ds(i * chunk_rows, chunk_rows) for i in range(groups // chunk)]
+    per_half = groups // HALVES
+    order = [HALVES * q + h for h in range(HALVES) for q in range(per_half)]
+    pieces = [pl.ds(g * group_rows, group_rows) for g in order]
     first_loads = [
         (w_in_hbm.at[0], w_in_ref),
         (b_in_hbm, b_in_ref),
@@ -147,32 +148,112 @@
     density_cols = jnp.transpose(jnp.broadcast_to(w_density_ref[...], (LANES, hid)))
     heads = jnp.concatenate([w_color_ref[...].astype(BF16), density_cols.astype(BF16)], axis=1)
     b_color = b_color_ref[...]
-    for c in range(groups // chunk):
-        rays = chunk * LANES
-        sample_loads[c].wait()
-        x = samples_ref[c * chunk * group_rows : (c + 1) * chunk * group_rows].reshape(rays, K * F)
-        for pair in range(K // 2):
-            part = x[:, pair * LANES : (pair + 1) * LANES]
-            part_high = part.astype(BF16)
-            part_low = (part - part_high.astype(F32)).astype(BF16)
-            both = jnp.concatenate([part_high, part_low, part_high], axis=1)
-            act = jnp.maximum(dot(both, pair_w) + pair_b, 0.0).astype(BF16)
-            for half in range(2):
-                k = 2 * pair + half
-                out = dot(act[:, half * hid : (half + 1) * hid], heads)
-                color = (out[:, :channels] + b_color).astype(BF16)
-                before = out[:, channels:].reshape(chunk, LANES, LANES)
-                for g in range(chunk):
-                    colors_ref[c * chunk + g, k * LANES : (k + 1) * LANES, :] = color[
-                        g * LANES : (g + 1) * LANES
-                    ]
-                density_ref[k, c * chunk : (c + 1) * chunk, :] = jnp.sum(
-                    jnp.where(eye, before, 0.0), axis=1
-                )
+    chunk = 2
+
+    def project(h):
+        for c in range(per_half // chunk):
+            rays = chunk * LANES
+            cells = []
+            for q in range(c * chunk, (c + 1) * chunk):
+                sample_loads[h * per_half + q].wait()
+                start = (HALVES * q + h) * group_rows
+                cells.append(samples_ref[start : start + group_rows].reshape(LANES, K * F))
+            x = jnp.concatenate(cells, axis=0)
+            for pair in range(K // 2):
+                part = x[:, pair * LANES : (pair + 1) * LANES]
+                part_high = part.astype(BF16)
+                part_low = (part - part_high.astype(F32)).astype(BF16)
+                both = jnp.concatenate([part_high, part_low, part_high], axis=1)
+                act = jnp.maximum(dot(both, pair_w) + pair_b, 0.0).astype(BF16)
+                for half in range(2):
+                    k = 2 * pair + half
+                    out = dot(act[:, half * hid : (half + 1) * hid], heads)
+                    color = (out[:, :channels] + b_color).astype(BF16)
+                    before = out[:, channels:].reshape(chunk, LANES, LANES)
+                    for q in range(chunk):
+                        colors_ref[h, c * chunk + q, k * LANES : (k + 1) * LANES, :] = color[
+                            q * LANES : (q + 1) * LANES
+                        ]
+                    density_ref[h, k, c * chunk : (c + 1) * chunk, :] = jnp.sum(
+                        jnp.where(eye, before, 0.0), axis=1
+                    )
+
+    def send_depth(h):
+        density = []
+        for k in range(K):
+            z = density_ref[h, k] + b_density_ref[0]
+            soft = jnp.maximum(z, 0.0) + jnp.log1p(jnp.exp(-jnp.abs(z)))
+            density.append(jnp.where(live[h] > k, soft, 0.0))
+        depths_ref[h, me] = density[0] + density[1] + density[2] + density[3]
+        if h == 0:
+            pl.semaphore_wait(
+                barrier, slabs + not_first.astype(jnp.int32) + not_last.astype(jnp.int32)
+            )
+
+        def send(shift, carry):
+            pltpu.make_async_remote_copy(
+                src_ref=depths_ref.at[h, me],
+                dst_ref=depths_ref.at[h, me],
+                send_sem=depth_send.at[h],
+                recv_sem=depth_recv.at[h],
+                device_id=(lax.rem(me + shift, slabs), tile),
+                device_id_type=MESH,
+            ).start()
+            return carry
+
+        lax.fori_loop(1, slabs, send, 0)
+        return density
+
+    def weigh(h, density):
+        peers = depths_ref.at[h, pl.ds(0, slabs - 1)]
+        pltpu.make_async_copy(peers, peers, depth_recv.at[h]).wait()
+        total = depths_ref[h, 0]
+        prefix = jnp.where(me > 0, total, 0.0)
+        for s in range(1, slabs):
+            one = depths_ref[h, s]
+            total = total + one
+            prefix = prefix + jnp.where(s < me, one, 0.0)
+        front = prefix / total
+        ahead = front
+        for k in range(K):
+            scaled = density[k] / total
+            weight_ref[h, k] = jnp.exp(-ahead) * (1.0 - jnp.exp(-scaled))
+            ahead = ahead + scaled
+        return front
+
+    def send_part(owner):
+        pltpu.make_async_remote_copy(
+            src_ref=sent_ref.at[owner],
+            dst_ref=parts_ref.at[me],
+            send_sem=part_send,
+            recv_sem=part_recv,
+            device_id=(owner, tile),
+            device_id_type=MESH,
+        ).start()
+
+    strips = LANES // strip_rays
+
+    def scatter(h):
+        for i in range(per_half):
+            q = lax.rem(me // (strips * HALVES) + i, per_half)
+            diag = [
+                jnp.where(eye, weight_ref[h, k, pl.ds(q, 1), :], 0.0).astype(BF16)
+                for k in range(K)
+            ]
+            image = dot(jnp.concatenate(diag, axis=1), colors_ref[h, q]).astype(BF16)
+            first = strips * (HALVES * q + h)
+            sent_ref[pl.ds(first, strips)] = image.reshape(strips, strip_rays, channels)
+            for j in range(strips):
+                owner = first + j
+                if i > 0:
+                    send_part(owner)
+                else:
+                    pl.when(owner != me)(functools.partial(send_part, owner))
+
+    project(0)
 
     for load in last_loads:
         load.wait()
-
     spread = (
         lax.rem(lax.broadcasted_iota(jnp.int32, (cols, LANES), 1), cols)
         == lax.broadcasted_iota(jnp.int32, (cols, LANES), 0)
@@ -186,32 +267,20 @@
         == lax.broadcasted_iota(jnp.int32, (rows, rows), 1)
     ).astype(BF16)
     by_row = dot_last(row_eye, counts_ref[...].astype(F32).astype(BF16)).astype(BF16)
-    live = dot(by_row, spread).reshape(groups, group_rows, LANES)
-    live = jnp.sum(jnp.where(own_lane, live, 0.0), axis=1)
-
-    density = []
-    for k in range(K):
-        z = density_ref[k] + b_density_ref[0]
-        soft = jnp.maximum(z, 0.0) + jnp.log1p(jnp.exp(-jnp.abs(z)))
-        density.append(jnp.where(live > k, soft, 0.0))
-    depths_ref[me] = density[0] + density[1] + density[2] + density[3]
-
-    pl.semaphore_wait(
-        barrier, slabs + not_first.astype(jnp.int32) + not_last.astype(jnp.int32)
-    )
-
-    def send_depth(shift, carry):
-        pltpu.make_async_remote_copy(
-            src_ref=depths_ref.at[me],
-            dst_ref=depths_ref.at[me],
-            send_sem=depth_send,
-            recv_sem=depth_recv,
-            device_id=(lax.rem(me + shift, slabs), tile),
-            device_id_type=MESH,
-        ).start()
-        return carry
-
-    lax.fori_loop(1, slabs, send_depth, 0)
+    spread_counts = dot(by_row, spread).reshape(per_half, HALVES, group_rows, LANES)
+    live = [
+        jnp.sum(jnp.where(own_lane, spread_counts[:, h], 0.0), axis=1) for h in range(HALVES)
+    ]
+
+    densities = [send_depth(0)]
+    for h in range(1, HALVES):
+        project(h)
+        densities.append(send_depth(h))
+    fronts = []
+    for h in range(HALVES):
+        fronts.append(weigh(h, densities[h]))
+        scatter(h)
+    parts_ref[me] = sent_ref[me]
 
     for taps, conv in ((taps_a, conv_a_ref), (taps_b, conv_b_ref)):
         for r in range(3):
@@ -220,48 +289,9 @@
                     r, s
                 ]
 
-    peers = depths_ref.at[pl.ds(0, slabs - 1)]
-    pltpu.make_async_copy(peers, peers, depth_recv).wait()
-    total = depths_ref[0]
-    prefix = jnp.where(me > 0, depths_ref[0], 0.0)
-    for s in range(1, slabs):
-        one = depths_ref[s]
-        total = total + one
-        prefix = prefix + jnp.where(s < me, one, 0.0)
-    front = prefix / total
-    ahead = front
-    for k in range(K):
-        scaled = density[k] / total
-        weight_ref[k] = jnp.exp(-ahead) * (1.0 - jnp.exp(-scaled))
-        ahead = ahead + scaled
-
-    def send_part(owner):
-        pltpu.make_async_remote_copy(
-            src_ref=sent_ref.at[owner],
-            dst_ref=parts_ref.at[me],
-            send_sem=part_send,
-            recv_sem=part_recv,
-            device_id=(owner, tile),
-            device_id_type=MESH,
-        ).start()
-
-    strips = LANES // strip_rays
-    place = lax.rem(me, strips)
-    for i in range(groups):
-        g = lax.rem(me // strips + i, groups)
-        diag = [
-            jnp.where(eye, weight_ref[k, pl.ds(g, 1), :], 0.0).astype(BF16) for k in range(K)
-        ]
-        image = dot(jnp.concatenate(diag, axis=1), colors_ref[g]).astype(BF16)
-        sent_ref[pl.ds(strips * g, strips)] = image.reshape(strips, strip_rays, channels)
-        for j in range(strips):
-            if i > 0:
-                send_part(strips * g + j)
-            elif j > 0:
-                send_part(strips * g + lax.rem(place + j, strips))
-    parts_ref[me] = sent_ref[me]
-
-    laid = jnp.where(own_lane, front[:, None, :], 0.0).reshape(rows, LANES)
+    laid = jnp.stack(
+        [jnp.where(own_lane, front[:, None, :], 0.0) for front in fronts], axis=1
+    ).reshape(rows, LANES)
     first = laid.astype(BF16)
     rest = laid - first.astype(F32)
     second = rest.astype(BF16)
@@ -362,8 +392,9 @@
     decoded = convolve(hidden_map.astype(BF16), taps_b, bias_b_ref[...].reshape(1, 1, channels))
     decoded_ref[...] = decoded[:, :cols].astype(BF16)
 
-    peers = depths_ref.at[pl.ds(0, slabs - 1)]
-    pltpu.make_async_copy(peers, peers, depth_send).wait()
+    for h in range(HALVES):
+        peers = depths_ref.at[h, pl.ds(0, slabs - 1)]
+        pltpu.make_async_copy(peers, peers, depth_send.at[h]).wait()
     peers = parts_ref.at[pl.ds(0, slabs - 1)]
     pltpu.make_async_copy(peers, peers, part_send).wait()
     across.wait_send()
@@ -402,7 +433,7 @@
     smem = pl.BlockSpec(memory_space=pltpu.SMEM)
     hbm = pl.BlockSpec(memory_space=pl.ANY)
     dma = pltpu.SemaphoreType.DMA
-    pieces = rows * cols // (2 * LANES)
+    per_half = groups // HALVES
     decoded, front = pl.pallas_call(
         functools.partial(render_kernel, slabs),
         out_shape=(
@@ -425,16 +456,16 @@
             pltpu.VMEM((1, channels), F32),
             pltpu.VMEM((3 * channels, 3 * channels), BF16),
             pltpu.VMEM((3 * channels, 3 * channels), BF16),
-            pltpu.VMEM((K, groups, LANES), F32),
-            pltpu.VMEM((groups, K * LANES, channels), BF16),
-            pltpu.VMEM((K, groups, LANES), F32),
-            pltpu.VMEM((slabs, groups, LANES), F32),
+            pltpu.VMEM((HALVES, K, per_half, LANES), F32),
+            pltpu.VMEM((HALVES, per_half, K * LANES, channels), BF16),
+            pltpu.VMEM((HALVES, K, per_half, LANES), F32),
+            pltpu.VMEM((HALVES, slabs, per_half, LANES), F32),
             pltpu.VMEM((slabs, strip * cols, channels), BF16),
             pltpu.VMEM((slabs, strip * cols, channels), BF16),
             pltpu.VMEM((2, strip + 4, cols, channels), BF16),
-            dma((10 + pieces,)),
-            dma,
-            dma,
+            dma((10 + groups,)),
+            dma((HALVES,)),
+            dma((HALVES,)),
             dma,
             dma,
             dma((5,)),

time: 26.5 us -> 25.8 us (0.974)
  Pallas kernels: 22.9 us -> 22.3 us
    pallas_call x1, Pallas kernels: 22.9 us -> 22.3 us  [body(): pl.pallas_call(functools.partial(render_kernel, slabs), out_shape=(jax.Sh...]
where the time goes in v3:
time: 25.8 us; the launch traced here: 25.6 us
  Pallas kernels  22.3 us (86%)
  local copies, waits for them, and re-layouts  1.93 us (7%)
  between operations  1.3 us (5%)
    pallas_call x1, Pallas kernels, body(): pl.pallas_call(functools.partial(render_kernel, slabs), out_shape=(jax.Sh...  22.3 us
    unnamed x4, local copies, waits for them, and re-layouts  1.93 us

profile of v3, /device:TPU:9, one launch (start us, length us, event | category | flops | bytes accessed | tf_op | source)
XLA Modules:
  0.0 25.6 jit_solution(16724499962968287770)
XLA Ops:
  1.3 22.3 %shard_map.131 = (bf16[4,16,128]{2,1,0:T(8,128)(2,1)}, f32[1,16,64]{2,1,0:T(8,128)}) custom-call(f32[1,64,16,256]{3,2,1,0:T(8,128)} %samples_hbm.1, s32[1,16,64]{2,1,0:T(8,128)} %bitcast.4, f32[1,64,256]{2,1,0:T(8,128)} %w_in_hbm.1, f32[1,256]{1,0:T(1,128)} %b_in_hbm.1, f32[1,256,128]{2,1,0:T(8,128)} %w_color_hbm.1, f32[1,128]{1,0:T(1,128)} %b_color_hbm.1, ...), custom_call_target="tpu_custom_call" | custom-call | tf_op jit(solution)/shard_map/pallas_call | solution.py:437
  23.6 0.0 copy-start
  23.6 1.3 %copy.17 = bf16[4,16,128]{2,1,0:T(8,128)(2,1)} copy(bf16[4,16,128]{2,1,0:T(8,128)(2,1)} %get-tuple-element.8) | data formatting | bytes 32768
  24.9 0.0 copy-done
  25.0 0.6 %copy.18 = f32[1,64,16]{1,2,0:T(8,128)} copy(f32[1,64,16]{1,2,0:T(8,128)S(1)} %bitcast.5) | data formatting | bytes 8192
Async XLA Ops:
  23.6 1.3 %copy-start = (f32[1,16,64]{2,1,0:T(8,128)S(1)}, f32[1,16,64]{2,1,0:T(8,128)}, u32[]{:S(2)}) copy-start(f32[1,16,64]{2,1,0:T(8,128)} %get-tuple-element.5) | copy-start | bytes 12292

commit v4 on v3

--- a/solution.py
+++ b/solution.py
@@ -11,6 +11,7 @@
 K = 4
 LANES = 128
 HALVES = 2
+PLANES = 4
 MESH = pl.DeviceIdType.MESH
 BF16 = jnp.bfloat16
 F32 = jnp.float32
@@ -33,7 +34,7 @@
     w_color_hbm,
     b_color_hbm,
     w_density_hbm,
-    b_density_ref,
+    b_density_hbm,
     conv_a_hbm,
     bias_a_hbm,
     conv_b_hbm,
@@ -47,6 +48,7 @@
     w_color_ref,
     b_color_ref,
     w_density_ref,
+    b_density_ref,
     conv_a_ref,
     bias_a_ref,
     conv_b_ref,
@@ -59,12 +61,16 @@
     depths_ref,
     sent_ref,
     parts_ref,
+    held_ref,
+    sums_ref,
     field_ref,
     load_sems,
     depth_send,
     depth_recv,
     part_send,
     part_recv,
+    sum_send,
+    sum_recv,
     edge_send,
     edge_recv,
 ):
@@ -81,8 +87,18 @@
     not_first = me > 0
     not_last = me < slabs - 1
 
+    plane = slabs // PLANES
+    my_plane, my_spot = me // plane, lax.rem(me, plane)
+    strips = LANES // strip_rays
+    plane_groups = plane // strips
+    folds = PLANES // HALVES
     per_half = groups // HALVES
-    order = [HALVES * q + h for h in range(HALVES) for q in range(per_half)]
+    order = [
+        (HALVES * fold + h) * plane_groups + r
+        for h in range(HALVES)
+        for fold in range(folds)
+        for r in range(plane_groups)
+    ]
     pieces = [pl.ds(g * group_rows, group_rows) for g in order]
     first_loads = [
         (w_in_hbm.at[0], w_in_ref),
@@ -95,6 +111,7 @@
         (counts_hbm.at[0], counts_ref),
         (conv_a_hbm, conv_a_ref),
         (conv_b_hbm, conv_b_ref),
+        (b_density_hbm, b_density_ref),
         (bias_a_hbm, bias_a_ref),
         (bias_b_hbm, bias_b_ref),
     ]
@@ -156,7 +173,7 @@
             cells = []
             for q in range(c * chunk, (c + 1) * chunk):
                 sample_loads[h * per_half + q].wait()
-                start = (HALVES * q + h) * group_rows
+                start = order[h * per_half + q] * group_rows
                 cells.append(samples_ref[start : start + group_rows].reshape(LANES, K * F))
             x = jnp.concatenate(cells, axis=0)
             for pair in range(K // 2):
@@ -221,34 +238,62 @@
             ahead = ahead + scaled
         return front
 
-    def send_part(owner):
+    def send_part(h, spot):
         pltpu.make_async_remote_copy(
-            src_ref=sent_ref.at[owner],
-            dst_ref=parts_ref.at[me],
-            send_sem=part_send,
-            recv_sem=part_recv,
-            device_id=(owner, tile),
+            src_ref=sent_ref.at[h, spot],
+            dst_ref=parts_ref.at[h, my_spot],
+            send_sem=part_send.at[h],
+            recv_sem=part_recv.at[h],
+            device_id=(my_plane * plane + spot, tile),
             device_id_type=MESH,
         ).start()
 
-    strips = LANES // strip_rays
-
     def scatter(h):
-        for i in range(per_half):
-            q = lax.rem(me // (strips * HALVES) + i, per_half)
-            diag = [
-                jnp.where(eye, weight_ref[h, k, pl.ds(q, 1), :], 0.0).astype(BF16)
-                for k in range(K)
-            ]
-            image = dot(jnp.concatenate(diag, axis=1), colors_ref[h, q]).astype(BF16)
-            first = strips * (HALVES * q + h)
-            sent_ref[pl.ds(first, strips)] = image.reshape(strips, strip_rays, channels)
+        for i in range(1, plane_groups + 1):
+            r = lax.rem(my_spot // strips + i, plane_groups)
+            for fold in range(folds):
+                q = fold * plane_groups + r
+                diag = [
+                    jnp.where(eye, weight_ref[h, k, pl.ds(q, 1), :], 0.0).astype(BF16)
+                    for k in range(K)
+                ]
+                image = dot(jnp.concatenate(diag, axis=1), colors_ref[h, q]).astype(BF16)
+                image = image.reshape(strips, strip_rays, channels)
+                for j in range(strips):
+                    sent_ref[h, strips * r + j, fold] = image[j]
             for j in range(strips):
-                owner = first + j
-                if i > 0:
-                    send_part(owner)
+                spot = strips * r + j
+                if i < plane_groups:
+                    send_part(h, spot)
                 else:
-                    pl.when(owner != me)(functools.partial(send_part, owner))
+                    pl.when(spot != my_spot)(functools.partial(send_part, h, spot))
+        parts_ref[h, my_spot] = sent_ref[h, my_spot]
+
+    def forward(h):
+        peers = parts_ref.at[h, pl.ds(0, plane - 1)]
+        pltpu.make_async_copy(peers, peers, part_recv.at[h]).wait()
+        for fold in range(folds):
+            part = parts_ref[h, 0, fold].astype(F32)
+            for s in range(1, plane):
+                part = part + parts_ref[h, s, fold].astype(F32)
+            held_ref[h, fold] = part.astype(BF16)
+            owner = HALVES * fold + h
+
+            def keep(fold=fold):
+                sums_ref[my_plane] = held_ref[h, fold]
+
+            def send(fold=fold, owner=owner):
+                pltpu.make_async_remote_copy(
+                    src_ref=held_ref.at[h, fold],
+                    dst_ref=sums_ref.at[my_plane],
+                    send_sem=sum_send,
+                    recv_sem=sum_recv,
+                    device_id=(owner * plane + my_spot, tile),
+                    device_id_type=MESH,
+                ).start()
+
+            pl.when(owner != my_plane)(send)
+            pl.when(owner == my_plane)(keep)
 
     project(0)
 
@@ -267,9 +312,13 @@
         == lax.broadcasted_iota(jnp.int32, (rows, rows), 1)
     ).astype(BF16)
     by_row = dot_last(row_eye, counts_ref[...].astype(F32).astype(BF16)).astype(BF16)
-    spread_counts = dot(by_row, spread).reshape(per_half, HALVES, group_rows, LANES)
+    spread_counts = dot(by_row, spread).reshape(folds, HALVES, plane_groups, group_rows, LANES)
     live = [
-        jnp.sum(jnp.where(own_lane, spread_counts[:, h], 0.0), axis=1) for h in range(HALVES)
+        jnp.sum(
+            jnp.where(own_lane, spread_counts[:, h].reshape(per_half, group_rows, LANES), 0.0),
+            axis=1,
+        )
+        for h in range(HALVES)
     ]
 
     densities = [send_depth(0)]
@@ -280,7 +329,8 @@
     for h in range(HALVES):
         fronts.append(weigh(h, densities[h]))
         scatter(h)
-    parts_ref[me] = sent_ref[me]
+    for h in range(HALVES):
+        forward(h)
 
     for taps, conv in ((taps_a, conv_a_ref), (taps_b, conv_b_ref)):
         for r in range(3):
@@ -290,7 +340,13 @@
                 ]
 
     laid = jnp.stack(
-        [jnp.where(own_lane, front[:, None, :], 0.0) for front in fronts], axis=1
+        [
+            jnp.where(own_lane, front[:, None, :], 0.0).reshape(
+                folds, plane_groups, group_rows, LANES
+            )
+            for front in fronts
+        ],
+        axis=1,
     ).reshape(rows, LANES)
     first = laid.astype(BF16)
     rest = laid - first.astype(F32)
@@ -298,11 +354,11 @@
     third = (rest - second.astype(F32)).astype(BF16)
     front_ref[0] = dot_last(spread, first) + dot_last(spread, second) + dot_last(spread, third)
 
-    peers = parts_ref.at[pl.ds(0, slabs - 1)]
-    pltpu.make_async_copy(peers, peers, part_recv).wait()
-    image = parts_ref[0].astype(F32)
-    for s in range(1, slabs):
-        image = image + parts_ref[s].astype(F32)
+    peers = sums_ref.at[pl.ds(0, PLANES - 1)]
+    pltpu.make_async_copy(peers, peers, sum_recv).wait()
+    image = sums_ref[0].astype(F32)
+    for s in range(1, PLANES):
+        image = image + sums_ref[s].astype(F32)
     image = image.astype(BF16).reshape(strip, cols, channels)
 
     field_ref[0, 2 : 2 + strip] = image
@@ -395,8 +451,11 @@
     for h in range(HALVES):
         peers = depths_ref.at[h, pl.ds(0, slabs - 1)]
         pltpu.make_async_copy(peers, peers, depth_send.at[h]).wait()
-    peers = parts_ref.at[pl.ds(0, slabs - 1)]
-    pltpu.make_async_copy(peers, peers, part_send).wait()
+        peers = parts_ref.at[h, pl.ds(0, plane - 1)]
+        pltpu.make_async_copy(peers, peers, part_send.at[h]).wait()
+    pltpu.make_async_copy(
+        sums_ref.at[pl.ds(0, PLANES - 1)], sums_ref.at[pl.ds(0, PLANES - 1)], sum_send
+    ).wait()
     across.wait_send()
 
     @pl.when(not_first)
@@ -430,7 +489,6 @@
     groups = rows * cols // LANES
     strip = rows // slabs
     vmem = pl.BlockSpec(memory_space=pltpu.VMEM)
-    smem = pl.BlockSpec(memory_space=pltpu.SMEM)
     hbm = pl.BlockSpec(memory_space=pl.ANY)
     dma = pltpu.SemaphoreType.DMA
     per_half = groups // HALVES
@@ -440,7 +498,7 @@
             jax.ShapeDtypeStruct((strip, cols, channels), BF16),
             jax.ShapeDtypeStruct((1, cols, rows), F32),
         ),
-        in_specs=[hbm] * 7 + [smem] + [hbm] * 4,
+        in_specs=[hbm] * 12,
         out_specs=(vmem, vmem),
         scratch_shapes=[
             pltpu.VMEM((rows, cols, width), F32),
@@ -450,6 +508,7 @@
             pltpu.VMEM(w_color.shape[1:], F32),
             pltpu.VMEM((1, channels), F32),
             pltpu.VMEM((1, hid), F32),
+            pltpu.SMEM((1,), F32),
             pltpu.VMEM(conv_a.shape, BF16),
             pltpu.VMEM((1, channels), F32),
             pltpu.VMEM(conv_b.shape, BF16),
@@ -460,10 +519,14 @@
             pltpu.VMEM((HALVES, per_half, K * LANES, channels), BF16),
             pltpu.VMEM((HALVES, K, per_half, LANES), F32),
             pltpu.VMEM((HALVES, slabs, per_half, LANES), F32),
-            pltpu.VMEM((slabs, strip * cols, channels), BF16),
-            pltpu.VMEM((slabs, strip * cols, channels), BF16),
+            pltpu.VMEM((HALVES, slabs // PLANES, PLANES // HALVES, strip * cols, channels), BF16),
+            pltpu.VMEM((HALVES, slabs // PLANES, PLANES // HALVES, strip * cols, channels), BF16),
+            pltpu.VMEM((HALVES, PLANES // HALVES, strip * cols, channels), BF16),
+            pltpu.VMEM((PLANES, strip * cols, channels), BF16),
             pltpu.VMEM((2, strip + 4, cols, channels), BF16),
-            dma((10 + groups,)),
+            dma((11 + groups,)),
+            dma((HALVES,)),
+            dma((HALVES,)),
             dma((HALVES,)),
             dma((HALVES,)),
             dma,

time: 25.8 us -> 26.5 us (1.027)
  the two profiles are of different devices: /device:TPU:9 before, /device:TPU:0 now
where the time goes in v4:
time: 26.5 us; the launch traced here: 26.2 us
  Pallas kernels  23 us (87%)
  local copies, waits for them, and re-layouts  1.93 us (7%)
  between operations  1.3 us (5%)
    pallas_call x1, Pallas kernels, body(): pl.pallas_call(functools.partial(render_kernel, slabs), out_shape=(jax.Sh...  23 us
    unnamed x4, local copies, waits for them, and re-layouts  1.93 us

profile of v4, /device:TPU:0, one launch (start us, length us, event | category | flops | bytes accessed | tf_op | source)
XLA Modules:
  0.0 26.2 jit_solution(17624946696334014446)
XLA Ops:
  1.3 23.0 %shard_map.131 = (bf16[4,16,128]{2,1,0:T(8,128)(2,1)}, f32[1,16,64]{2,1,0:T(8,128)}) custom-call(f32[1,64,16,256]{3,2,1,0:T(8,128)} %samples_hbm.1, s32[1,16,64]{2,1,0:T(8,128)} %bitcast.4, f32[1,64,256]{2,1,0:T(8,128)} %w_in_hbm.1, f32[1,256]{1,0:T(1,128)} %b_in_hbm.1, f32[1,256,128]{2,1,0:T(8,128)} %w_color_hbm.1, f32[1,128]{1,0:T(1,128)} %b_color_hbm.1, ...), custom_call_target="tpu_custom_call" | custom-call | tf_op jit(solution)/shard_map/pallas_call | solution.py:495
  24.3 0.0 copy-start
  24.3 1.3 %copy.17 = bf16[4,16,128]{2,1,0:T(8,128)(2,1)} copy(bf16[4,16,128]{2,1,0:T(8,128)(2,1)} %get-tuple-element.8) | data formatting | bytes 32768
  25.6 0.0 copy-done
  25.7 0.6 %copy.18 = f32[1,64,16]{1,2,0:T(8,128)} copy(f32[1,64,16]{1,2,0:T(8,128)S(1)} %bitcast.5) | data formatting | bytes 8192
Async XLA Ops:
  24.3 1.3 %copy-start = (f32[1,16,64]{2,1,0:T(8,128)S(1)}, f32[1,16,64]{2,1,0:T(8,128)}, u32[]{:S(2)}) copy-start(f32[1,16,64]{2,1,0:T(8,128)} %get-tuple-element.5) | copy-start | bytes 12292

commit v5 on v3

--- a/solution.py
+++ b/solution.py
@@ -135,20 +135,16 @@
 
     for load in first_loads:
         load.wait()
-    w_in = w_in_ref[...]
-    high = w_in.astype(BF16)
-    low = (w_in - high.astype(F32)).astype(BF16)
-    blank = jnp.zeros_like(high)
-    even = [high, blank, high, blank, low, blank]
-    odd = [blank, high, blank, high, blank, low]
+    w_in = w_in_ref[...].astype(BF16)
+    blank = jnp.zeros_like(w_in)
     pair_w = jnp.concatenate(
-        [jnp.concatenate(even, axis=0), jnp.concatenate(odd, axis=0)], axis=1
+        [jnp.concatenate([w_in, blank], axis=0), jnp.concatenate([blank, w_in], axis=0)], axis=1
     )
     pair_b = jnp.concatenate([b_in_ref[...], b_in_ref[...]], axis=1)
     density_cols = jnp.transpose(jnp.broadcast_to(w_density_ref[...], (LANES, hid)))
     heads = jnp.concatenate([w_color_ref[...].astype(BF16), density_cols.astype(BF16)], axis=1)
     b_color = b_color_ref[...]
-    chunk = 2
+    chunk = min(4, per_half)
 
     def project(h):
         for c in range(per_half // chunk):
@@ -160,11 +156,8 @@
                 cells.append(samples_ref[start : start + group_rows].reshape(LANES, K * F))
             x = jnp.concatenate(cells, axis=0)
             for pair in range(K // 2):
-                part = x[:, pair * LANES : (pair + 1) * LANES]
-                part_high = part.astype(BF16)
-                part_low = (part - part_high.astype(F32)).astype(BF16)
-                both = jnp.concatenate([part_high, part_low, part_high], axis=1)
-                act = jnp.maximum(dot(both, pair_w) + pair_b, 0.0).astype(BF16)
+                part = x[:, pair * LANES : (pair + 1) * LANES].astype(BF16)
+                act = jnp.maximum(dot(part, pair_w) + pair_b, 0.0).astype(BF16)
                 for half in range(2):
                     k = 2 * pair + half
                     out = dot(act[:, half * hid : (half + 1) * hid], heads)
@@ -408,6 +401,10 @@
     def _():
         for copy in down:
             copy.wait_send()
+
+
+def stay(array):
+    return pltpu.with_memory_space_constraint(array, pltpu.HBM)
 
 
 def body(
@@ -431,7 +428,7 @@
     strip = rows // slabs
     vmem = pl.BlockSpec(memory_space=pltpu.VMEM)
     smem = pl.BlockSpec(memory_space=pltpu.SMEM)
-    hbm = pl.BlockSpec(memory_space=pl.ANY)
+    hbm = pl.BlockSpec(memory_space=pltpu.HBM)
     dma = pltpu.SemaphoreType.DMA
     per_half = groups // HALVES
     decoded, front = pl.pallas_call(
@@ -472,21 +469,21 @@
             dma((5,)),
         ],
         compiler_params=pltpu.CompilerParams(
-            collective_id=0, has_side_effects=True, vmem_limit_bytes=60 * 2**20
+            collective_id=0, has_side_effects=True, vmem_limit_bytes=32 * 2**20
         ),
     )(
-        samples,
-        jnp.swapaxes(counts, 1, 2),
-        w_in,
-        b_in,
-        w_color,
-        b_color,
-        w_density,
+        stay(samples),
+        stay(jnp.swapaxes(counts, 1, 2)),
+        stay(w_in),
+        stay(b_in),
+        stay(w_color),
+        stay(b_color),
+        stay(w_density),
         b_density,
-        conv_a,
-        bias_a.reshape(1, channels),
-        conv_b,
-        bias_b.reshape(1, channels),
+        stay(conv_a),
+        stay(bias_a.reshape(1, channels)),
+        stay(conv_b),
+        stay(bias_b.reshape(1, channels)),
     )
     return decoded, jnp.swapaxes(front, 1, 2)
 

time: 25.8 us -> 23.6 us (0.915)
  Pallas kernels: 22.3 us -> 21 us
  local copies, waits for them, and re-layouts: 1.93 us -> 1.21 us
    pallas_call x1, Pallas kernels: 22.3 us -> 21 us  [body(): pl.pallas_call(functools.partial(render_kernel, slabs), out_shape=(jax.Sh...]
    unnamed x4 -> x2, local copies, waits for them, and re-layouts: 1.93 us -> 1.21 us
where the time goes in v5:
time: 23.6 us; the launch traced here: 23.5 us
  Pallas kernels  21 us (89%)
  between operations  1.29 us (5%)
  local copies, waits for them, and re-layouts  1.21 us (5%)
    pallas_call x1, Pallas kernels, body(): pl.pallas_call(functools.partial(render_kernel, slabs), out_shape=(jax.Sh...  21 us
    unnamed x2, local copies, waits for them, and re-layouts  1.21 us

profile of v5, /device:TPU:9, one launch (start us, length us, event | category | flops | bytes accessed | tf_op | source)
XLA Modules:
  0.0 23.5 jit_solution(817991567604374552)
XLA Ops:
  1.3 21.0 %shard_map.131 = (bf16[4,16,128]{2,1,0:T(8,128)(2,1)S(1)}, f32[1,16,64]{2,1,0:T(8,128)S(1)}) custom-call(f32[1,64,16,256]{3,2,1,0:T(8,128)} %samples_hbm.1, s32[1,16,64]{2,1,0:T(8,128)} %bitcast.5, f32[1,64,256]{2,1,0:T(8,128)} %w_in_hbm.1, f32[1,256]{1,0:T(1,128)} %b_in_hbm.1, f32[1,256,128]{2,1,0:T(8,128)} %w_color_hbm.1, f32[1,128]{1,0:T(1,128)} %b_color_hbm.1, ...), custom_call_target="tpu_custom_call" | custom-call | tf_op jit(solution)/shard_map/pallas_call | solution.py:434
  22.3 0.6 %copy.17 = bf16[4,16,128]{2,1,0:T(8,128)(2,1)} copy(bf16[4,16,128]{2,1,0:T(8,128)(2,1)S(1)} %get-tuple-element.8) | data formatting | bytes 32768
  22.9 0.6 %copy.18 = f32[1,64,16]{1,2,0:T(8,128)} copy(f32[1,64,16]{1,2,0:T(8,128)S(1)} %bitcast.4) | data formatting | bytes 8192

commit v6 on v5

--- a/solution.py
+++ b/solution.py
@@ -87,12 +87,12 @@
     first_loads = [
         (w_in_hbm.at[0], w_in_ref),
         (b_in_hbm, b_in_ref),
+        (counts_hbm.at[0], counts_ref),
         (w_color_hbm.at[0], w_color_ref),
         (w_density_hbm, w_density_ref),
         (b_color_hbm, b_color_ref),
     ]
     last_loads = [
-        (counts_hbm.at[0], counts_ref),
         (conv_a_hbm, conv_a_ref),
         (conv_b_hbm, conv_b_ref),
         (bias_a_hbm, bias_a_ref),
@@ -114,11 +114,8 @@
     def greet(slab, tile_at):
         pl.semaphore_signal(barrier, inc=1, device_id=(slab, tile_at), device_id_type=MESH)
 
-    def greet_slab(shift, carry):
+    for shift in range(1, slabs):
         greet(lax.rem(me + shift, slabs), tile)
-        return carry
-
-    lax.fori_loop(1, slabs, greet_slab, 0)
     greet(me, other)
 
     @pl.when(not_first)
@@ -183,7 +180,7 @@
                 barrier, slabs + not_first.astype(jnp.int32) + not_last.astype(jnp.int32)
             )
 
-        def send(shift, carry):
+        for shift in range(1, slabs):
             pltpu.make_async_remote_copy(
                 src_ref=depths_ref.at[h, me],
                 dst_ref=depths_ref.at[h, me],
@@ -192,9 +189,6 @@
                 device_id=(lax.rem(me + shift, slabs), tile),
                 device_id_type=MESH,
             ).start()
-            return carry
-
-        lax.fori_loop(1, slabs, send, 0)
         return density
 
     def weigh(h, density):
@@ -243,10 +237,6 @@
                 else:
                     pl.when(owner != me)(functools.partial(send_part, owner))
 
-    project(0)
-
-    for load in last_loads:
-        load.wait()
     spread = (
         lax.rem(lax.broadcasted_iota(jnp.int32, (cols, LANES), 1), cols)
         == lax.broadcasted_iota(jnp.int32, (cols, LANES), 0)
@@ -265,6 +255,7 @@
         jnp.sum(jnp.where(own_lane, spread_counts[:, h], 0.0), axis=1) for h in range(HALVES)
     ]
 
+    project(0)
     densities = [send_depth(0)]
     for h in range(1, HALVES):
         project(h)
@@ -275,6 +266,8 @@
         scatter(h)
     parts_ref[me] = sent_ref[me]
 
+    for load in last_loads:
+        load.wait()
     for taps, conv in ((taps_a, conv_a_ref), (taps_b, conv_b_ref)):
         for r in range(3):
             for s in range(3):

time: 23.6 us -> 23.6 us (level)
  no operation moved by 1% of the time
where the time goes in v6:
time: 23.6 us; the launch traced here: 23.5 us
  Pallas kernels  21 us (89%)
  between operations  1.29 us (5%)
  local copies, waits for them, and re-layouts  1.21 us (5%)
    pallas_call x1, Pallas kernels, body(): pl.pallas_call(functools.partial(render_kernel, slabs), out_shape=(jax.Sh...  21 us
    unnamed x2, local copies, waits for them, and re-layouts  1.21 us

profile of v6, /device:TPU:9, one launch (start us, length us, event | category | flops | bytes accessed | tf_op | source)
XLA Modules:
  0.0 23.5 jit_solution(7854644782959318256)
XLA Ops:
  1.3 21.0 %shard_map.131 = (bf16[4,16,128]{2,1,0:T(8,128)(2,1)S(1)}, f32[1,16,64]{2,1,0:T(8,128)S(1)}) custom-call(f32[1,64,16,256]{3,2,1,0:T(8,128)} %samples_hbm.1, s32[1,16,64]{2,1,0:T(8,128)} %bitcast.5, f32[1,64,256]{2,1,0:T(8,128)} %w_in_hbm.1, f32[1,256]{1,0:T(1,128)} %b_in_hbm.1, f32[1,256,128]{2,1,0:T(8,128)} %w_color_hbm.1, f32[1,128]{1,0:T(1,128)} %b_color_hbm.1, ...), custom_call_target="tpu_custom_call" | custom-call | tf_op jit(solution)/shard_map/pallas_call | solution.py:427
  22.3 0.6 %copy.17 = bf16[4,16,128]{2,1,0:T(8,128)(2,1)} copy(bf16[4,16,128]{2,1,0:T(8,128)(2,1)S(1)} %get-tuple-element.8) | data formatting | bytes 32768
  22.9 0.6 %copy.18 = f32[1,64,16]{1,2,0:T(8,128)} copy(f32[1,64,16]{1,2,0:T(8,128)S(1)} %bitcast.4) | data formatting | bytes 8192
